TPU v7x, 256 devices: a whole 4x4x8 slice. The times are simulated.
256 devices in a mesh: snode: 64 (over x, z, core), rows: 4 (over y).
Axes of the slice: x: 4, y: 4, z: 8, core: 2. Of those that a mesh axis runs over, the one named last changes fastest.
Arguments:
- root_covariance: bfloat16 [4096, 4096], P('rows'), may hold values from -6 to 6
- ancestors: int32 [64, 4], replicated, may hold values from 0 to 7, as said below
- parents: int32 [64], replicated, may hold values from 0 to 63
- panel_first: bfloat16 [64, 2048, 512], P('snode', 'rows'), may hold values from -0.125 to 0.125
- inverse_first: bfloat16 [64, 512, 512], P('snode', 'rows'), may hold values from -6 to 6
- panel_upper: bfloat16 [64, 512, 512], P('snode', 'rows'), may hold values from -0.125 to 0.125
- panel_lower: bfloat16 [64, 2048, 512], P('snode', 'rows'), may hold values from -0.125 to 0.125
- inverse_second: bfloat16 [64, 512, 512], P('snode', 'rows'), may hold values from -6 to 6
Outputs:
- offdiag_first: bfloat16 [64, 2048, 512], P('snode', 'rows')
- diagonal_first: bfloat16 [64, 512, 512], P('snode', 'rows')
- offdiag_upper: bfloat16 [64, 512, 512], P('snode', 'rows')
- offdiag_lower: bfloat16 [64, 2048, 512], P('snode', 'rows')
- diagonal_second: bfloat16 [64, 512, 512], P('snode', 'rows')
Inputs may be any that keep to these rules, and one draw needn't show every extreme that they name: `ancestors`: each row holds 4 different root block numbers.
All inputs are finite; a program needn't handle non-finite values.
Results may differ from a plain program's by a relative error of at most 0.018.
Values may be sent and summed in bfloat16 or wider, within the bound.
No kernel may reach another device: no remote copies, remote signals or barrier semaphores. Data moves between devices by JAX's collectives and lax.ppermute only.
A program may use at most 128 MiB of HBM per device.

v0:
```python
import jax
import jax.numpy as jnp
from jax import lax
from jax.sharding import PartitionSpec as P


def ancestor_term(root_rows, chosen, panel_full):
    block_width = panel_full.shape[1]
    local_blocks = root_rows.shape[0] // block_width
    root_count = root_rows.shape[1] // block_width
    anc_count = chosen.shape[0]
    row_parts = lax.axis_size("rows")
    first_block = lax.axis_index("rows") * local_blocks
    tile_rows = jnp.take(
        root_rows.reshape(local_blocks, block_width, root_count, block_width), chosen, axis=2
    )
    tile_rows = tile_rows.reshape(local_blocks, block_width, anc_count * block_width)
    owned_mask = chosen[:, None] == first_block + jnp.arange(local_blocks, dtype=jnp.int32)[None, :]
    products = jnp.einsum("lbc,cd->lbd", tile_rows, panel_full, preferred_element_type=jnp.float32)
    picked = owned_mask.astype(jnp.float32)
    placed = jnp.sum(picked[:, :, None, None] * products[None], axis=1)
    return lax.psum_scatter(
        placed.reshape(
            panel_full.shape[0] // row_parts * lax.axis_size("rows"), block_width
        ).astype(jnp.bfloat16),
        "rows",
        scatter_dimension=0,
        tiled=True,
    ).astype(jnp.float32)


def on_device(
    root_covariance,
    ancestors,
    parents,
    panel_first,
    inverse_first,
    panel_upper,
    panel_lower,
    inverse_second,
):
    owner_node = lax.axis_index("snode")
    chosen_first = lax.dynamic_slice_in_dim(ancestors, owner_node, 1, 0)[0]
    parent = lax.dynamic_slice_in_dim(parents, owner_node, 1, 0)[0]
    chosen_second = lax.dynamic_slice_in_dim(ancestors, parent, 1, 0)[0]
    panel_local = panel_first[0]
    panel_whole = lax.all_gather(panel_local, "rows", axis=0, tiled=True)
    offdiag_one = (-ancestor_term(root_covariance, chosen_first, panel_whole)).astype(jnp.bfloat16)
    first_fix = lax.psum_scatter(
        jnp.dot(panel_local.T, offdiag_one, preferred_element_type=jnp.float32).astype(
            jnp.bfloat16
        ),
        "rows",
        scatter_dimension=0,
        tiled=True,
    ).astype(jnp.float32)
    diagonal_one = (inverse_first[0].astype(jnp.float32) - first_fix).astype(jnp.bfloat16)
    upper_local = panel_upper[0]
    lower_local = panel_lower[0]
    upper_whole, lower_whole = (
        lax.all_gather(upper_local, "rows", axis=0, tiled=True),
        lax.all_gather(lower_local, "rows", axis=0, tiled=True),
    )
    root_part = ancestor_term(root_covariance, chosen_second, lower_whole)
    stacked = jnp.concatenate([offdiag_one, diagonal_one], axis=0)
    node_count = lax.axis_size("snode")
    slice_width = stacked.shape[0] * stacked.shape[1] // node_count
    spread = lax.all_to_all(
        stacked.reshape(node_count, slice_width), "snode", split_axis=0, concat_axis=0, tiled=True
    )
    onward = jnp.take(spread, parents, axis=0)
    delivered = lax.all_to_all(onward, "snode", split_axis=0, concat_axis=0, tiled=True).reshape(
        stacked.shape
    )
    anc_rows = offdiag_one.shape[0]
    parent_offdiag = delivered[:anc_rows]
    parent_diagonal = delivered[anc_rows:]
    lower_value = (
        jnp.dot(parent_offdiag, upper_whole, preferred_element_type=jnp.float32) + root_part
    )
    cross_part = lax.psum_scatter(
        jnp.dot(parent_offdiag.T, lower_local, preferred_element_type=jnp.float32).astype(
            jnp.bfloat16
        ),
        "rows",
        scatter_dimension=0,
        tiled=True,
    ).astype(jnp.float32)
    upper_value = (
        jnp.dot(parent_diagonal, upper_whole, preferred_element_type=jnp.float32) + cross_part
    )
    offdiag_up = (-upper_value).astype(jnp.bfloat16)
    offdiag_low = (-lower_value).astype(jnp.bfloat16)
    diag_parts = jnp.dot(upper_local.T, offdiag_up, preferred_element_type=jnp.float32) + jnp.dot(
        lower_local.T, offdiag_low, preferred_element_type=jnp.float32
    )
    second_fix = lax.psum_scatter(
        diag_parts.astype(jnp.bfloat16), "rows", scatter_dimension=0, tiled=True
    ).astype(jnp.float32)
    diagonal_two = (inverse_second[0].astype(jnp.float32) - second_fix).astype(jnp.bfloat16)
    return (
        offdiag_one[None],
        diagonal_one[None],
        offdiag_up[None],
        offdiag_low[None],
        diagonal_two[None],
    )


def solution(mesh):
    placed = (
        P("rows", None),
        P(),
        P(),
        P("snode", "rows", None),
        P("snode", "rows", None),
        P("snode", "rows", None),
        P("snode", "rows", None),
        P("snode", "rows", None),
    )
    return jax.shard_map(
        on_device,
        mesh=mesh,
        in_specs=placed,
        out_specs=(
            P("snode", "rows", None),
            P("snode", "rows", None),
            P("snode", "rows", None),
            P("snode", "rows", None),
            P("snode", "rows", None),
        ),
        check_vma=False,
    )
```

profile of v0, /device:TPU:6, one launch (start us, length us, event | category | flops | bytes accessed | tf_op | source)
XLA Modules:
  0.0 286.9 jit_solution(11736538995320025496)
XLA Ops:
  8.0 1.2 dynamic_slice.10
  10.5 12.2 %copy.79 = bf16[128,8,8,512]{3,2,1,0:T(8,128)(2,1)} copy(bf16[128,8,8,512]{3,1,2,0:T(8,128)(2,1)} %bitcast.68) | data formatting | bytes 16777216
  22.7 9.9 %copy.59 = bf16[2,512,8,512]{3,1,0,2:T(8,128)(2,1)} copy(bf16[2,512,8,512]{3,2,1,0:T(8,128)(2,1)} %bitcast.65) | data formatting | bytes 16777216 | tf_op jit(solution)/shard_map/reshape | solution.py:15
  33.5 6.2 %gather_fusion.1 = bf16[4,2,512,512]{3,2,1,0:T(8,128)(2,1)} fusion(bf16[2,512,8,512]{3,1,0,2:T(8,128)(2,1)} %copy.59, s32[1024]{0:T(1024)S(1)} %pad_clamp_fusion.2), kind=kCustom, calls=%fused_computation.clone | custom fusion | bytes 8388624 | tf_op jit(solution)/shard_map/jit(_take)/gather | solution.py:14
  39.7 4.6 %select_bitcast_fusion.1 = bf16[2,512,4,512]{3,1,0,2:T(8,128)(2,1)} fusion(bf16[4,2,512,512]{3,2,1,0:T(8,128)(2,1)} %gather_fusion.1, pred[4]{0:T(512)(128)(4,1)S(1)} %get-tuple-element.45), kind=kLoop, calls=%fused_computation.6 | loop fusion | flops 2097152 | bytes 8388612 | tf_op jit(solution)/shard_map/jit(_take)/select_n | solution.py:14
  44.4 7.3 %copy.60 = bf16[2,512,4,512]{1,3,2,0:T(8,128)(2,1)} copy(bf16[2,512,4,512]{3,1,0,2:T(8,128)(2,1)} %select_bitcast_fusion.1) | data formatting | bytes 8388608 | tf_op jit(solution)/shard_map/jit(_take)/select_n | solution.py:14
  51.7 5.2 %fusion.2 = f32[2,512,512]{2,1,0:T(8,128)S(1)} fusion(bf16[2,512,2048]{1,2,0:T(8,128)(2,1)} %bitcast.66, bf16[1,2048,512]{2,1,0:T(8,128)(2,1)} %all-gather.6.cloned.1.call-done), kind=kOutput, calls=%fused_computation.9 | convolution fusion | flops 2147483648 | bytes 8388608 | tf_op jit(solution)/shard_map/lbc,cd->lbd/dot_general | solution.py:19
  57.0 2.4 multiply_reduce_fusion.1
  60.2 6.2 %gather_fusion.2 = bf16[4,2,512,512]{3,2,1,0:T(8,128)(2,1)} fusion(bf16[2,512,8,512]{3,1,0,2:T(8,128)(2,1)} %copy.59, s32[1024]{0:T(1024)S(1)} %pad_clamp_fusion), kind=kCustom, calls=%fused_computation.1.clone | custom fusion | bytes 8388624 | tf_op jit(solution)/shard_map/jit(_take)/gather | solution.py:14
  66.4 28.2 %reduce-scatter.10.cloned.1.call-done = bf16[512,512]{1,0:T(8,128)(2,1)} async-done(((bf16[2048,512]{1,0:T(8,128)(2,1)}), bf16[512,512]{1,0:T(8,128)(2,1)}) %reduce-scatter.10.cloned.1.call-update) | async-done | bytes 524304 | tf_op jit(solution)/shard_map/reduce_scatter | solution.py:22
  94.6 1.5 fusion.8
  97.2 4.6 %select_bitcast_fusion = bf16[2,512,4,512]{3,1,0,2:T(8,128)(2,1)} fusion(bf16[4,2,512,512]{3,2,1,0:T(8,128)(2,1)} %gather_fusion.2, pred[4]{0:T(512)(128)(4,1)S(1)} %get-tuple-element.44), kind=kLoop, calls=%fused_computation.5 | loop fusion | flops 2097152 | bytes 8388612 | tf_op jit(solution)/shard_map/jit(_take)/select_n | solution.py:14
  102.0 7.3 %copy.67 = bf16[2,512,4,512]{1,3,2,0:T(8,128)(2,1)} copy(bf16[2,512,4,512]{3,1,0,2:T(8,128)(2,1)} %select_bitcast_fusion) | data formatting | bytes 8388608 | tf_op jit(solution)/shard_map/jit(_take)/select_n | solution.py:14
  109.3 20.4 %all-gather.8.cloned.1.call-done = bf16[1,2048,512]{2,1,0:T(8,128)(2,1)} async-done(((bf16[1,512,512]{2,1,0:T(8,128)(2,1)}), bf16[1,2048,512]{2,1,0:T(8,128)(2,1)}) %all-gather.8.cloned.1.call-update) | async-done | bytes 2097168 | tf_op jit(solution)/shard_map/all_gather | solution.py:62
  129.8 5.2 %fusion = f32[2,512,512]{2,1,0:T(8,128)S(1)} fusion(bf16[2,512,2048]{1,2,0:T(8,128)(2,1)} %bitcast.67, bf16[1,2048,512]{2,1,0:T(8,128)(2,1)} %all-gather.8.cloned.1.call-done), kind=kOutput, calls=%fused_computation.7 | convolution fusion | flops 2147483648 | bytes 8388608 | tf_op jit(solution)/shard_map/lbc,cd->lbd/dot_general | solution.py:19
  135.0 2.4 multiply_reduce_fusion
  138.4 18.5 %reduce-scatter.16.cloned.1.call-done = bf16[128,512]{1,0:T(8,128)(2,1)} async-done(((bf16[512,512]{1,0:T(8,128)(2,1)}), bf16[128,512]{1,0:T(8,128)(2,1)}) %reduce-scatter.16.cloned.1.call-update) | async-done | bytes 131088
  156.9 1.0 copy.75
  159.1 4.6 %reduce.5 = bf16[64,5120]{1,0:T(8,128)(2,1)S(1)} reduce(bf16[64,1,5120]{2,1,0:T(2,128)(2,1)S(1)} %all_to_all.16, bf16[]{:T(256)} %broadcast.134), dimensions={1}, to_apply=%all_to_all.16.reduce_sub_computation | reduce | bytes 1310722 | tf_op jit(solution)/shard_map/all_to_all | solution.py:68
  163.6 1.3 reshape.192
  165.0 10.7 %all-to-all-start = ((bf16[64,2,2560]{2,1,0:T(2,128)(2,1)}), bf16[64,2,2560]{2,1,0:T(2,128)(2,1)S(1)}, u32[]{:S(2)}, u32[]{:S(2)}) async-start(bf16[64,2,2560]{2,1,0:T(2,128)(2,1)} %reshape.192), calls=%async_computation.1 | async-start | bytes 1310720 | tf_op jit(solution)/shard_map/all_to_all | solution.py:68
  175.8 19.2 %all-to-all-done = bf16[64,2,2560]{2,1,0:T(2,128)(2,1)S(1)} async-done(((bf16[64,2,2560]{2,1,0:T(2,128)(2,1)}), bf16[64,2,2560]{2,1,0:T(2,128)(2,1)S(1)}, u32[]{:S(2)}, u32[]{:S(2)}) %all-to-all-start) | async-done | bytes 655392 | tf_op jit(solution)/shard_map/all_to_all | solution.py:68
  196.8 1.1 reduce.6
  198.4 26.2 %all_to_all.19 = bf16[64,2,2560]{2,1,0:T(2,128)(2,1)S(1)} all-to-all(bf16[64,2,2560]{2,1,0:T(2,128)(2,1)S(1)} %reshape.194), channel_id=1, replica_groups=mesh['snode'=64,'rows'=4] {'snode'}, dimensions={0} | all-to-all | bytes 1310720 | tf_op jit(solution)/shard_map/all_to_all | solution.py:72
  225.1 3.9 %reduce.1 = bf16[64,5120]{1,0:T(8,128)(2,1)S(1)} reduce(bf16[64,1,5120]{2,1,0:T(2,128)(2,1)S(1)} %reshape.195, bf16[]{:T(256)} %constant.47), dimensions={1}, to_apply=%all_to_all.15.reduce_sub_computation | reduce | bytes 1310722 | tf_op jit(solution)/shard_map/all_to_all | solution.py:72
  229.8 1.2 convolution_convert_fusion
  231.2 14.7 %all-gather.1 = bf16[1,512,512]{2,1,0:T(8,128)(2,1)S(1)} all-gather(bf16[1,128,512]{2,1,0:T(8,128)(2,1)S(1)} %copy-done.3), channel_id=3, replica_groups=mesh['snode'=64,'rows'=4] {'rows'}, dimensions={1}, use_global_device_ids=true | all-gather | bytes 655360 | tf_op jit(solution)/shard_map/all_gather | solution.py:61
  245.9 1.5 fusion.5
  247.4 4.4 %reduce-scatter.12.cloned.1.call-done = bf16[128,512]{1,0:T(8,128)(2,1)} async-done(((bf16[512,512]{1,0:T(8,128)(2,1)}), bf16[128,512]{1,0:T(8,128)(2,1)}) %reduce-scatter.12.cloned.1.call-update) | async-done | bytes 131088 | tf_op jit(solution)/shard_map/reduce_scatter | solution.py:81
  251.9 1.1 fusion.10
  255.7 22.5 %reduce-scatter.18.cloned.1.call-done = bf16[128,512]{1,0:T(8,128)(2,1)} async-done(((bf16[512,512]{1,0:T(8,128)(2,1)}), bf16[128,512]{1,0:T(8,128)(2,1)}) %reduce-scatter.18.cloned.1.call-update) | async-done | bytes 131088
  278.2 1.0 copy.77
  (68 shorter events, 12.3 us)
Async XLA Ops:
  7.2 44.6 %all-gather.6.cloned.1.call-start = ((), (), s32[]{:S(2)}) async-start(), calls=%async_computation.10 | async-start | bytes 2621440 | tf_op jit(solution)/shard_map/all_gather | solution.py:47
  7.9 86.7 %reduce-scatter.10.cloned.1.call-start = ((), (), s32[]{:S(2)}) async-start(), calls=%async_computation.7 | async-start | bytes 2621440 | tf_op jit(solution)/shard_map/reduce_scatter | solution.py:22
  22.7 10.6 %copy-start.8 = (s32[64,4]{0,1:T(4,128)S(1)}, s32[64,4]{0,1:T(4,128)}, u32[]{:S(2)}) copy-start(s32[64,4]{0,1:T(4,128)} %param.11) | copy-start | bytes 3076
  59.4 70.3 %all-gather.8.cloned.1.call-start = ((), (), s32[]{:S(2)}) async-start(), calls=%async_computation.11 | async-start | bytes 2621440 | tf_op jit(solution)/shard_map/all_gather | solution.py:62
  60.1 96.8 %reduce-scatter.16.cloned.1.call-start = ((), (), s32[]{:S(2)}) async-start(), calls=%async_computation.12 | async-start | bytes 655360
  60.2 34.4 %copy-start.5 = (bf16[1,512,512]{2,1,0:T(8,128)(2,1)S(1)}, bf16[1,512,512]{2,1,0:T(8,128)(2,1)}, u32[]{:S(2)}) copy-start(bf16[1,512,512]{2,1,0:T(8,128)(2,1)} %param.13) | copy-start | bytes 1572868
  97.2 148.7 %reduce-scatter.14.cloned.1.call-start = ((), (), s32[]{:S(2)}) async-start(), calls=%async_computation.9 | async-start | bytes 2621440 | tf_op jit(solution)/shard_map/reduce_scatter | solution.py:22
  97.2 4.7 %copy-start.6 = (bf16[1,128,512]{2,1,0:T(8,128)(2,1)S(1)}, bf16[1,128,512]{2,1,0:T(8,128)(2,1)}, u32[]{:S(2)}) copy-start(bf16[1,128,512]{2,1,0:T(8,128)(2,1)} %param.14) | copy-start | bytes 393220
  135.0 2.5 copy-start.1
  157.9 17.8 %copy-start.9 = (s32[64]{0:T(128)S(1)}, s32[64]{0:T(128)}, u32[]{:S(2)}) copy-start(s32[64]{0:T(128)} %param.12) | copy-start | bytes 772
  165.0 30.0 %all-to-all-start = ((bf16[64,2,2560]{2,1,0:T(2,128)(2,1)}), bf16[64,2,2560]{2,1,0:T(2,128)(2,1)S(1)}, u32[]{:S(2)}, u32[]{:S(2)}) async-start(bf16[64,2,2560]{2,1,0:T(2,128)(2,1)} %reshape.192), calls=%async_computation.1 | async-start | bytes 1310720 | tf_op jit(solution)/shard_map/all_to_all | solution.py:68
  175.7 76.2 %reduce-scatter.12.cloned.1.call-start = ((), (), s32[]{:S(2)}) async-start(), calls=%async_computation.8 | async-start | bytes 655360 | tf_op jit(solution)/shard_map/reduce_scatter | solution.py:81
  197.9 31.9 %copy-start = (bf16[1,512,512]{2,1,0:T(8,128)(2,1)S(1)}, bf16[1,512,512]{2,1,0:T(8,128)(2,1)}, u32[]{:S(2)}) copy-start(bf16[1,512,512]{2,1,0:T(8,128)(2,1)} %param.16) | copy-start | bytes 1572868
  224.6 6.6 %copy-start.3 = (bf16[1,128,512]{2,1,0:T(8,128)(2,1)S(1)}, bf16[1,128,512]{2,1,0:T(8,128)(2,1)}, u32[]{:S(2)}) copy-start(bf16[1,128,512]{2,1,0:T(8,128)(2,1)} %param.15) | copy-start | bytes 393220
  231.1 47.1 %reduce-scatter.18.cloned.1.call-start = ((), (), s32[]{:S(2)}) async-start(), calls=%async_computation.13 | async-start | bytes 655360
  245.9 8.9 %copy-start.7 = (bf16[1,128,512]{2,1,0:T(8,128)(2,1)S(1)}, bf16[1,128,512]{2,1,0:T(8,128)(2,1)}, u32[]{:S(2)}) copy-start(bf16[1,128,512]{2,1,0:T(8,128)(2,1)} %param.17) | copy-start | bytes 393220
  247.4 32.6 %copy-start.2 = (bf16[512,512]{1,0:T(8,128)(2,1)}, bf16[512,512]{1,0:T(8,128)(2,1)S(1)}, u32[]{:S(2)}) copy-start(bf16[512,512]{1,0:T(8,128)(2,1)S(1)} %fusion.5) | copy-start | bytes 1572868
  253.0 27.0 %copy-start.4 = (bf16[128,512]{1,0:T(8,128)(2,1)}, bf16[128,512]{1,0:T(8,128)(2,1)S(1)}, u32[]{:S(2)}) copy-start(bf16[128,512]{1,0:T(8,128)(2,1)S(1)} %fusion.10) | copy-start | bytes 393220
Sparse Core Ops, SparseCore 0:
  9.8 36.3 all-gather.5
  59.5 35.0 reduce-scatter.9
  96.6 33.1 all-gather.7
  132.9 23.9 reduce-scatter.15
  159.5 31.9 reduce-scatter.13
  231.2 20.6 reduce-scatter.11
  255.0 23.2 reduce-scatter.17
where the time goes:
time: 288 us; the launch traced here: 287 us
  waiting for transfers between devices  115 us (40%)
  local copies, waits for them, and re-layouts  62.3 us (22%)
  blocking collectives  40.9 us (14%)
  other arithmetic  25 us (9%)
  matrix products  16.6 us (6%)
  between operations  16.4 us (6%)
  starting transfers between devices  11 us (4%)
    unnamed x9, waiting for transfers between devices  42.4 us
    reduce_scatter x2, waiting for transfers between devices, ancestor_term(): lax.psum_scatter(placed.reshape(panel_full.shape[0] // row_parts * lax.ax...  28.2 us
    all_to_all x1, blocking collectives, on_device(): lax.all_to_all(onward, 'snode', split_axis=0, concat_axis=0, tiled=True)  26.2 us
    unnamed x34, local copies, waits for them, and re-layouts  21.2 us
    all_gather x1, waiting for transfers between devices, on_device(): lax.all_gather(lower_local, 'rows', axis=0, tiled=True)  20.4 us
    all_to_all x1, waiting for transfers between devices, on_device(): lax.all_to_all(stacked.reshape(node_count, slice_width), 'snode', split_a...  19.2 us
    all_gather x1, blocking collectives, on_device(): lax.all_gather(upper_local, 'rows', axis=0, tiled=True)  14.7 us
    select_n x2, local copies, waits for them, and re-layouts, ancestor_term(): jnp.take(root_rows.reshape(local_blocks, block_width, root_count, block_w...  14.6 us
  transfers between devices with their start and end apart: 8, of which 6 were waited for; matrix products, arithmetic and copies ran while one was open for 32% of the time, Pallas kernels for 0%

commit v1 on v0

v1 whole, which is shorter than its diff:
```python
import jax
import jax.numpy as jnp
from jax import lax
from jax.experimental import pallas as pl
from jax.experimental.pallas import tpu as pltpu
from jax.sharding import PartitionSpec as P

BF = jnp.bfloat16
F32 = jnp.float32
VMEM_BYTES = 48 * 1024 * 1024


def vmem():
    return pl.BlockSpec(memory_space=pltpu.VMEM)


def shift(value, step):
    n = lax.axis_size("rows")
    return lax.ppermute(value, "rows", [(i, (i + step) % n) for i in range(n)])


def rows_dot(lhs, rhs):
    return lax.dot_general(lhs, rhs, (((0,), (0,)), ((), ())), preferred_element_type=F32)


def gather_rows(block):
    half = block.shape[0] // 2
    top, bottom = block[:half], block[half:]
    left_top = shift(top, 1)
    right_bottom = shift(bottom, -1)
    left_bottom = shift(bottom, 1)
    right_top = shift(top, -1)
    far_top = shift(left_top, 1)
    far_bottom = shift(right_bottom, -1)
    return (block, right_top, right_bottom, far_top, far_bottom, left_top, left_bottom)


def scatter_rows(next_two, before_two, next_a, next_b, before_a, before_b):
    from_left_two = shift(next_two, 1)
    from_right_two = shift(before_two, -1)
    left_b = shift(next_b, 1)
    right_a = shift(before_a, -1)
    left_a = shift(next_a + from_left_two, 1)
    right_b = shift(before_b + from_right_two, -1)
    return left_a, left_b, right_a, right_b


def near_kernel(ids, anc, p0, p1t, p1b, p3t, p3b, t0, t1, t3, out):
    block = pl.program_id(0)
    width = p0.shape[0]
    half = width // 2
    node, row = ids[0], ids[1]
    hits = [anc[node, lax.rem(row + d, 4)] == 2 * row + block for d in range(4)]

    @pl.when(hits[0] | hits[1] | hits[2] | hits[3])
    def _():
        total = jnp.dot(t0[...], p0[...], preferred_element_type=F32)
        for tile, top, bottom in ((t1, p1t, p1b), (t3, p3t, p3b)):
            total += jnp.dot(tile[:, :half], top[...], preferred_element_type=F32)
            total += jnp.dot(tile[:, half:], bottom[...], preferred_element_type=F32)
        out[...] = total


def first_kernel(ids, anc, p0, p1t, p1b, p2t, p2b, p3t, p3b, t2, near,
                 mine, next_a, next_b, two_a, two_b, before_a, before_b, prod, fix):
    block = pl.program_id(0)
    width = p0.shape[0]
    half = width // 2
    cut = next_a.shape[0]
    node, row = ids[0], ids[1]
    halves = ((p0.at[:half], p0.at[half:]), (p1t, p1b), (p2t, p2b), (p3t, p3b))
    targets = ((mine, None), (next_a, next_b), (two_a, two_b), (before_a, before_b))
    hits = [anc[node, lax.rem(row + d, 4)] == 2 * row + block for d in range(4)]

    @pl.when(block == 0)
    def _():
        fix[...] = jnp.zeros_like(fix)
        for a, b in targets:
            a[...] = jnp.zeros_like(a)
            if b is not None:
                b[...] = jnp.zeros_like(b)

    @pl.when(hits[0] | hits[1] | hits[2] | hits[3])
    def _():
        total = near[...]
        total += jnp.dot(t2[:, :half], p2t[...], preferred_element_type=F32)
        total += jnp.dot(t2[:, half:], p2b[...], preferred_element_type=F32)
        prod[...] = (-total).astype(BF)

    for d in range(4):
        a, b = targets[d]
        top, bottom = halves[d]

        @pl.when(hits[d])
        def _():
            if b is None:
                a[:width, :] = prod[...]
            else:
                a[...] = prod[:cut, :]
                b[: width - cut, :] = prod[cut:, :]
            fix[...] -= rows_dot(top[...], prod[:half, :]) + rows_dot(bottom[...], prod[half:, :])

    @pl.when(block == 1)
    def _():
        share = width // 4
        for d in range(4):
            start = pl.multiple_of(lax.rem(row + d, 4) * share, share)
            part = fix[pl.ds(start, share), :].astype(BF)
            a, b = targets[d]
            if b is None:
                a[width:, :] = part
            else:
                b[width - cut :, :] = part


def tile_spec(k, second):
    def index(l, ids, anc, *rest):
        node = rest[0][ids[0]] if second else ids[0]
        return l, anc[node, lax.rem(ids[1] + k, 4)]

    return pl.BlockSpec((512, 512), index)


def whole_spec(shape):
    return pl.BlockSpec(shape, lambda l, *_: (0,) * len(shape))


def near_products(ids, ancestors, pieces, root_rows):
    width = pieces[0].shape[0]
    return pl.pallas_call(
        near_kernel,
        out_shape=jax.ShapeDtypeStruct((2 * width, width), F32),
        grid_spec=pltpu.PrefetchScalarGridSpec(
            num_scalar_prefetch=2,
            grid=(2,),
            in_specs=[whole_spec(p.shape) for p in pieces]
            + [tile_spec(k, False) for k in (0, 1, 3)],
            out_specs=pl.BlockSpec((width, width), lambda l, *_: (l, 0)),
        ),
        compiler_params=pltpu.CompilerParams(vmem_limit_bytes=VMEM_BYTES),
        cost_estimate=pl.CostEstimate(
            flops=6 * width**3 * 2, bytes_accessed=6 << 20, transcendentals=0
        ),
        name="near_products",
    )(ids, ancestors, *pieces, *([root_rows] * 3))


def first_products(ids, ancestors, pieces, root_rows, near):
    width = pieces[0].shape[0]
    share = width // 4
    cut = (width + share) // 2
    shapes = [(width + share, width)] + [(cut, width)] * 6
    outs = [jax.ShapeDtypeStruct(s, BF) for s in shapes]
    return pl.pallas_call(
        first_kernel,
        out_shape=outs,
        grid_spec=pltpu.PrefetchScalarGridSpec(
            num_scalar_prefetch=2,
            grid=(2,),
            in_specs=[whole_spec(p.shape) for p in pieces]
            + [tile_spec(2, False), pl.BlockSpec((width, width), lambda l, *_: (l, 0))],
            out_specs=[whole_spec(s) for s in shapes],
            scratch_shapes=[pltpu.VMEM((width, width), BF), pltpu.VMEM((width, width), F32)],
        ),
        compiler_params=pltpu.CompilerParams(vmem_limit_bytes=VMEM_BYTES),
        cost_estimate=pl.CostEstimate(
            flops=4 * width**3 * 2, bytes_accessed=8 << 20, transcendentals=0
        ),
        name="first_products",
    )(ids, ancestors, *pieces, root_rows, near)


def second_kernel(ids, anc, parents, l0, l1, l2, l3, t0, t1, t2, t3,
                  mine, after, far, before, corr, prod):
    block = pl.program_id(0)
    row = ids[1]
    node = parents[ids[0]]
    lows = (l0, l1, l2, l3)
    outs = (mine, after, far, before)
    hits = [anc[node, lax.rem(row + d, 4)] == 2 * row + block for d in range(4)]

    @pl.when(block == 0)
    def _():
        corr[...] = jnp.zeros_like(corr)
        for out in outs:
            out[...] = jnp.zeros_like(out)

    @pl.when(hits[0] | hits[1] | hits[2] | hits[3])
    def _():
        total = None
        for tile, low in zip((t0, t1, t2, t3), lows):
            term = jnp.dot(tile[...], low[...], preferred_element_type=F32)
            total = term if total is None else total + term
        prod[...] = total.astype(BF)

    for d in range(4):

        @pl.when(hits[d])
        def _():
            outs[d][...] = prod[...]
            corr[...] += rows_dot(lows[d][...], prod[...])


def second_products(ids, ancestors, parents, lows, root_rows):
    width = lows[0].shape[1]
    square = (width, width)
    return pl.pallas_call(
        second_kernel,
        out_shape=[jax.ShapeDtypeStruct(square, BF)] * 4 + [jax.ShapeDtypeStruct(square, F32)],
        grid_spec=pltpu.PrefetchScalarGridSpec(
            num_scalar_prefetch=3,
            grid=(2,),
            in_specs=[whole_spec(square)] * 4 + [tile_spec(k, True) for k in range(4)],
            out_specs=[whole_spec(square)] * 5,
            scratch_shapes=[pltpu.VMEM(square, BF)],
        ),
        compiler_params=pltpu.CompilerParams(vmem_limit_bytes=VMEM_BYTES),
        cost_estimate=pl.CostEstimate(
            flops=6 * width**3 * 2, bytes_accessed=9 << 20, transcendentals=0
        ),
        name="second_products",
    )(ids, ancestors, parents, *lows, *([root_rows] * 4))


def settle_kernel(mine, left_a, left_b, right_a, right_b, inverse, off, diag, slices):
    width = off.shape[1]
    share = diag.shape[0]
    cut = left_a.shape[0]
    rest = width - cut
    nodes, deep, _ = slices.shape

    def total(m, x, y):
        return m.astype(F32) + x.astype(F32) + y.astype(F32)

    upper = total(mine[:cut, :], left_a[...], right_a[...])
    lower = total(mine[cut:width, :], left_b[:rest, :], right_b[:rest, :])
    off[:cut, :] = upper.astype(BF)
    off[cut:, :] = lower.astype(BF)
    value = inverse[...].astype(F32) + total(mine[width:, :], left_b[rest:, :], right_b[rest:, :])
    diag[...] = value.astype(BF)
    edge = cut // deep
    slices[:edge, :, :width] = upper.reshape(edge, deep, width).astype(BF)
    slices[edge:, :, :width] = lower.reshape(nodes - edge, deep, width).astype(BF)
    groups = share // deep
    for c in range(nodes // groups):
        part = value[:, c * 128 : (c + 1) * 128].reshape(groups, deep, 128)
        slices[c * groups : (c + 1) * groups, :, width:] = part.astype(BF)


def settle(mine, received, inverse, nodes):
    width = inverse.shape[1]
    share = inverse.shape[0]
    deep = width // nodes
    return pl.pallas_call(
        settle_kernel,
        out_shape=(
            jax.ShapeDtypeStruct((width, width), BF),
            jax.ShapeDtypeStruct((share, width), BF),
            jax.ShapeDtypeStruct((nodes, deep, width + share), BF),
        ),
        in_specs=[vmem()] * 6,
        out_specs=(vmem(),) * 3,
        compiler_params=pltpu.CompilerParams(vmem_limit_bytes=VMEM_BYTES),
        cost_estimate=pl.CostEstimate(flops=1 << 21, bytes_accessed=4 << 20, transcendentals=0),
        name="settle_first",
    )(mine, *received, inverse)


def pick_kernel(parents, held, onward):
    def step(i, carry):
        onward[i] = held[parents[i]]
        return carry

    lax.fori_loop(0, onward.shape[0], step, 0, unroll=8)


def pick(parents, held):
    return pl.pallas_call(
        pick_kernel,
        out_shape=jax.ShapeDtypeStruct(held.shape, held.dtype),
        in_specs=[pl.BlockSpec(memory_space=pltpu.SMEM), vmem()],
        out_specs=vmem(),
        compiler_params=pltpu.CompilerParams(vmem_limit_bytes=VMEM_BYTES),
        cost_estimate=pl.CostEstimate(flops=1 << 20, bytes_accessed=2 << 20, transcendentals=0),
        name="pick_parents",
    )(parents, held)


def last_kernel(ids, came, u0, u1, u2, u3, low, corr_in, off_part, keep_up, keep_diag,
                next_a, next_b, two_a, two_b, before_a, before_b, cross, corr, whole):
    nodes, deep, wide = came.shape
    width = low.shape[1]
    share = wide - width
    row = ids[1]
    for d, part in enumerate((u0, u1, u2, u3)):
        whole[lax.rem(row + d, 4)] = part[...]
    upper = whole[...].reshape(width, width)
    parent_off = came[:, :, :width].astype(F32).reshape(nodes * deep, width).astype(BF)
    groups = share // deep
    parent_diag = jnp.concatenate(
        [
            came[c * groups : (c + 1) * groups, :, width:].astype(F32).reshape(share, 128)
            for c in range(nodes // groups)
        ],
        axis=1,
    ).astype(BF)
    across = rows_dot(parent_off, low[...])
    cross[...] = across
    own = jnp.dot(parent_diag, upper, preferred_element_type=F32)
    lower = jnp.dot(parent_off, upper, preferred_element_type=F32)
    off_part[...] = lower
    corr[...] = (
        corr_in[...]
        + rows_dot(u0[...], own.astype(BF))
        + rows_dot(low[...], lower.astype(BF))
        + rows_dot(upper, across.astype(BF))
    )

    def rows_of(ref, d):
        start = pl.multiple_of(lax.rem(row + d, 4) * share, share)
        return ref[pl.ds(start, share), :]

    keep_up[...] = own + rows_of(cross, 0)
    keep_diag[...] = rows_of(corr, 0)
    for d, (a, b) in ((1, (next_a, next_b)), (2, (two_a, two_b)), (3, (before_a, before_b))):
        a[...] = rows_of(cross, d).astype(BF)
        b[...] = rows_of(corr, d).astype(BF)


def last_products(ids, came, ups, low, corr):
    width = low.shape[1]
    share = ups[0].shape[0]
    small = jax.ShapeDtypeStruct((share, width), BF)
    kept = jax.ShapeDtypeStruct((share, width), F32)
    return pl.pallas_call(
        last_kernel,
        out_shape=(jax.ShapeDtypeStruct((width, width), F32), kept, kept) + (small,) * 6,
        in_specs=[pl.BlockSpec(memory_space=pltpu.SMEM)] + [vmem()] * 7,
        out_specs=(vmem(),) * 9,
        scratch_shapes=[
            pltpu.VMEM((width, width), F32),
            pltpu.VMEM((width, width), F32),
            pltpu.VMEM((4, share, width), BF),
        ],
        compiler_params=pltpu.CompilerParams(vmem_limit_bytes=VMEM_BYTES),
        cost_estimate=pl.CostEstimate(
            flops=5 * width**3 * 2, bytes_accessed=6 << 20, transcendentals=0
        ),
        name="last_products",
    )(ids, came, *ups, low, corr)


def after(value, *others):
    return lax.optimization_barrier((value, *others))[0]


def spread_rows(block):
    return block, shift(block, -1), shift(block, 2), shift(block, 1)


def on_device(root_rows, ancestors, parents, panel_first, inverse_first, panel_upper, panel_lower,
              inverse_second):
    nodes = lax.axis_size("snode")
    ids = jnp.stack([lax.axis_index("snode"), lax.axis_index("rows")]).astype(jnp.int32)
    pieces = gather_rows(panel_first[0])
    near = near_products(ids, ancestors, pieces[:3] + pieces[5:], root_rows)
    mine, next_a, next_b, two_a, two_b, before_a, before_b = first_products(
        ids, ancestors, pieces, root_rows, near
    )
    received = scatter_rows(two_a, two_b, next_a, next_b, before_a, before_b)
    off_first, diag_first, slices = settle(mine, received, inverse_first[0], nodes)
    low, up = lax.optimization_barrier((panel_lower[0], panel_upper[0], off_first))[:2]
    lows, ups = spread_rows(low), spread_rows(up)
    spread = lax.all_to_all(slices, "snode", split_axis=0, concat_axis=0, tiled=True)
    own, to_next, to_far, to_before, corr = second_products(
        ids, ancestors, parents, lows, root_rows
    )
    picked, to_next, to_far, to_before, ups = lax.optimization_barrier(
        (pick(parents, spread), to_next, to_far, to_before, ups)
    )
    roots = (own, shift(to_next, 1), shift(to_far, 2), shift(to_before, -1))
    came = lax.all_to_all(picked, "snode", split_axis=0, concat_axis=0, tiled=True)
    off_part, keep_up, keep_diag, next_a, next_b, two_a, two_b, before_a, before_b = last_products(
        ids, came, ups, low, corr
    )
    left_a, left_b, right_a, right_b = scatter_rows(two_a, two_b, next_a, next_b, before_a, before_b)
    off_up = -(keep_up + left_a.astype(F32) + right_a.astype(F32))
    diag_second = (
        inverse_second[0].astype(F32) + keep_diag + left_b.astype(F32) + right_b.astype(F32)
    )
    off_low = off_part
    for part in roots:
        off_low = off_low + part.astype(F32)
    return (
        off_first[None],
        diag_first[None],
        off_up.astype(BF)[None],
        (-off_low).astype(BF)[None],
        diag_second.astype(BF)[None],
    )


def solution(mesh):
    split = P("snode", "rows", None)
    return jax.shard_map(
        on_device,
        mesh=mesh,
        in_specs=(P("rows", None), P(), P(), split, split, split, split, split),
        out_specs=(split,) * 5,
        check_vma=False,
    )
```

time: 288 us -> 162 us (0.56)
  starting transfers between devices: 11 us -> 68.3 us
  local copies, waits for them, and re-layouts: 62.3 us -> 5.85 us
  waiting for transfers between devices: 115 us -> 62.5 us
  blocking collectives: 40.9 us -> 0 us
  other arithmetic: 25 us -> 5.19 us
  Pallas kernels: 0 us -> 17.8 us
  matrix products: 16.6 us -> 0 us
  between operations: 16.4 us -> 0.82 us
    ppermute x0 -> x27, waiting for transfers between devices: none -> 48.7 us  [shift(): return lax.ppermute(value, 'rows', [(i, (i + step) % n) for i in range(n)])]
    ppermute x0 -> x27, starting transfers between devices: none -> 44.3 us  [shift(): return lax.ppermute(value, 'rows', [(i, (i + step) % n) for i in range(n)])]
    unnamed x9 -> x0, waiting for transfers between devices: 42.4 us -> none
    reduce_scatter x3 -> x0, waiting for transfers between devices: 32.6 us -> none  [the longest x2 28.2 us: ancestor_term(): lax.psum_scatter(placed.reshape(panel_full.shape[0] // row_parts * lax.ax...]
    all_to_all x1 -> x0, blocking collectives: 26.2 us -> none  [on_device(): lax.all_to_all(onward, 'snode', split_axis=0, concat_axis=0, tiled=True)]
    all_gather x2 -> x0, waiting for transfers between devices: 20.4 us -> none  [the longest x1 20.4 us: on_device(): lax.all_gather(lower_local, 'rows', axis=0, tiled=True)]
    pallas_call x0 -> x6, Pallas kernels: none -> 17.8 us  [the longest x1 4.84 us: second_products(): pl.pallas_call(second_kernel, out_shape=[jax.ShapeDtypeStruct(square, BF)...]
    dot_general x8 -> x0, matrix products: 16.6 us -> none  [the longest x2 10.4 us: ancestor_term(): jnp.einsum('lbc,cd->lbd', tile_rows, panel_full, preferred_element_type=j...]
  transfers between devices with their start and end apart: 8 -> 29, of which waited for: 6 -> 11; matrix products, arithmetic and copies ran while one was open for 32% -> 3% of each run, Pallas kernels for 0% -> 8%
where the time goes in v1:
time: 162 us; the launch traced here: 160 us
  starting transfers between devices  68.3 us (42%)
  waiting for transfers between devices  62.5 us (39%)
  Pallas kernels  17.8 us (11%)
  local copies, waits for them, and re-layouts  5.85 us (4%)
  other arithmetic  5.19 us (3%)
    ppermute x27, waiting for transfers between devices, shift(): return lax.ppermute(value, 'rows', [(i, (i + step) % n) for i in range(n)])  48.7 us
    ppermute x27, starting transfers between devices, shift(): return lax.ppermute(value, 'rows', [(i, (i + step) % n) for i in range(n)])  44.3 us
    all_to_all x1, waiting for transfers between devices, on_device(): lax.all_to_all(picked, 'snode', split_axis=0, concat_axis=0, tiled=True)  13.8 us
    all_to_all x1, starting transfers between devices, on_device(): lax.all_to_all(slices, 'snode', split_axis=0, concat_axis=0, tiled=True)  13.5 us
    all_to_all x1, starting transfers between devices, on_device(): lax.all_to_all(picked, 'snode', split_axis=0, concat_axis=0, tiled=True)  10.5 us
    pallas_call x1, Pallas kernels, second_products(): pl.pallas_call(second_kernel, out_shape=[jax.ShapeDtypeStruct(square, BF)...  4.84 us
    unnamed x17, local copies, waits for them, and re-layouts  4.78 us
    pallas_call x1, Pallas kernels, first_products(): pl.pallas_call(first_kernel, out_shape=outs, grid_spec=pltpu.PrefetchScal...  3.86 us
  transfers between devices with their start and end apart: 29, of which 11 were waited for; matrix products, arithmetic and copies ran while one was open for 3% of the time, Pallas kernels for 8%

profile of v1, /device:TPU:6, one launch (start us, length us, event | category | flops | bytes accessed | tf_op | source)
XLA Modules:
  0.0 160.4 jit_solution(14267034752679906475)
XLA Ops:
  1.7 3.1 %collective-permute-start.1 = (bf16[256,512]{1,0:T(8,128)(2,1)S(1)}, bf16[256,512]{1,0:T(8,128)(2,1)S(1)}, u32[]{:S(2)}, u32[]{:S(2)}) collective-permute-start(bf16[256,512]{1,0:T(8,128)(2,1)S(1)} %get-tuple-element.73), channel_id=1, source_target_pairs={{0,3},{1,0},{2,1},{3,2},{4,7},{5,4},{6,5},{7,6},{8,11},{9,8},{10,9... | collective-permute-start | bytes 786440 | tf_op jit(solution)/shard_map/ppermute | solution.py:19
  5.4 2.7 %collective-permute-start = (bf16[256,512]{1,0:T(8,128)(2,1)S(1)}, bf16[256,512]{1,0:T(8,128)(2,1)S(1)}, u32[]{:S(2)}, u32[]{:S(2)}) collective-permute-start(bf16[256,512]{1,0:T(8,128)(2,1)S(1)} %get-tuple-element.74), channel_id=1, source_target_pairs={{0,3},{1,0},{2,1},{3,2},{4,7},{5,4},{6,5},{7,6},{8,11},{9,8},{10,9... | collective-permute-start | bytes 786440 | tf_op jit(solution)/shard_map/ppermute | solution.py:19
  8.8 2.7 %collective-permute-done.1.p1b = bf16[256,512]{1,0:T(8,128)(2,1)S(1)} collective-permute-done((bf16[256,512]{1,0:T(8,128)(2,1)S(1)}, bf16[256,512]{1,0:T(8,128)(2,1)S(1)}, u32[]{:S(2)}, u32[]{:S(2)}) %collective-permute-start.1) | collective-permute-done | bytes 262176 | tf_op jit(solution)/shard_map/ppermute | solution.py:19
  11.5 3.7 %collective-permute-start.4 = (bf16[256,512]{1,0:T(8,128)(2,1)S(1)}, bf16[256,512]{1,0:T(8,128)(2,1)S(1)}, u32[]{:S(2)}, u32[]{:S(2)}) collective-permute-start(bf16[256,512]{1,0:T(8,128)(2,1)S(1)} %collective-permute-done.1.p1b), channel_id=1, source_target_pairs={{0,3},{1,0},{2,1},{3,2},{4,7},{5,4},{6,5},{7,6},{8,11},{9,8},{10,9... | collective-permute-start | bytes 786440 | tf_op jit(solution)/shard_map/ppermute | solution.py:19
  15.3 5.5 %collective-permute-done.5.p3b = bf16[256,512]{1,0:T(8,128)(2,1)S(1)} collective-permute-done((bf16[256,512]{1,0:T(8,128)(2,1)S(1)}, bf16[256,512]{1,0:T(8,128)(2,1)S(1)}, u32[]{:S(2)}, u32[]{:S(2)}) %collective-permute-start.5) | collective-permute-done | bytes 262176 | tf_op jit(solution)/shard_map/ppermute | solution.py:19
  21.9 3.6 %near_products.1.near = f32[1024,512]{1,0:T(8,128)S(1)} custom-call(s32[2]{0:T(128)S(1)} %pad_add_fusion.ids, s32[64,4]{1,0:T(8,128)S(1)} %copy.14.anc, bf16[512,512]{1,0:T(8,128)(2,1)S(1)} %bitcast.21, bf16[256,512]{1,0:T(8,128)(2,1)S(1)} %collective-permute-done.p1t, bf16[256,512]{1,0:T(8,128)(2,1)S(1)} %collective-permute-done.1.p1b, ...), custom_call_target="tpu_custom_call" | custom-call | flops 1610612736 | bytes 6291456 | tf_op jit(solution)/shard_map/near_products/pallas_call | solution.py:130
  26.9 3.9 %first_products.1 = (bf16[640,512]{1,0:T(8,128)(2,1)S(1)}, bf16[320,512]{1,0:T(8,128)(2,1)S(1)}, bf16[320,512]{1,0:T(8,128)(2,1)S(1)}, bf16[320,512]{1,0:T(8,128...) custom-call(s32[2]{0:T(128)S(1)} %pad_add_fusion.ids, ...), custom_call_target="tpu_custom_call" | custom-call | flops 1073741824 | bytes 8388608 | tf_op jit(solution)/shard_map/first_products/pallas_call | solution.py:154
  30.8 3.2 %collective-permute-start.10 = (bf16[320,512]{1,0:T(8,128)(2,1)S(1)}, bf16[320,512]{1,0:T(8,128)(2,1)S(1)}, u32[]{:S(2)}, u32[]{:S(2)}) collective-permute-start(bf16[320,512]{1,0:T(8,128)(2,1)S(1)} %get-tuple-element.45), channel_id=1, source_target_pairs={{0,3},{1,0},{2,1},{3,2},{4,7},{5,4},{6,5},{7,6},{8,11},{9,8},{10,9... | collective-permute-start | bytes 983048 | tf_op jit(solution)/shard_map/ppermute | solution.py:19
  34.1 3.2 %collective-permute-start.9 = (bf16[320,512]{1,0:T(8,128)(2,1)S(1)}, bf16[320,512]{1,0:T(8,128)(2,1)S(1)}, u32[]{:S(2)}, u32[]{:S(2)}) collective-permute-start(bf16[320,512]{1,0:T(8,128)(2,1)S(1)} %get-tuple-element.43), channel_id=1, source_target_pairs={{0,3},{1,0},{2,1},{3,2},{4,7},{5,4},{6,5},{7,6},{8,11},{9,8},{10,9... | collective-permute-start | bytes 983048 | tf_op jit(solution)/shard_map/ppermute | solution.py:19
  37.3 5.4 %collective-permute-done.6 = bf16[320,512]{1,0:T(8,128)(2,1)S(1)} collective-permute-done((bf16[320,512]{1,0:T(8,128)(2,1)S(1)}, bf16[320,512]{1,0:T(8,128)(2,1)S(1)}, u32[]{:S(2)}, u32[]{:S(2)}) %collective-permute-start.6) | collective-permute-done | bytes 327712 | tf_op jit(solution)/shard_map/ppermute | solution.py:19
  43.0 3.5 %collective-permute-start.11 = (bf16[320,512]{1,0:T(8,128)(2,1)S(1)}, bf16[320,512]{1,0:T(8,128)(2,1)S(1)}, u32[]{:S(2)}, u32[]{:S(2)}) collective-permute-start(bf16[320,512]{1,0:T(8,128)(2,1)S(1)} %add.40), channel_id=1, source_target_pairs={{0,3},{1,0},{2,1},{3,2},{4,7},{5,4},{6,5},{7,6},{8,11},{9,8},{10,9... | collective-permute-start | bytes 983048 | tf_op jit(solution)/shard_map/ppermute | solution.py:19
  46.4 3.3 %collective-permute-done.8.left_b = bf16[320,512]{1,0:T(8,128)(2,1)S(1)} collective-permute-done((bf16[320,512]{1,0:T(8,128)(2,1)S(1)}, bf16[320,512]{1,0:T(8,128)(2,1)S(1)}, u32[]{:S(2)}, u32[]{:S(2)}) %collective-permute-start.8) | collective-permute-done | bytes 327712 | tf_op jit(solution)/shard_map/ppermute | solution.py:19
  49.7 3.7 %collective-permute-done.7.left_a = bf16[320,512]{1,0:T(8,128)(2,1)S(1)} collective-permute-done((bf16[320,512]{1,0:T(8,128)(2,1)S(1)}, bf16[320,512]{1,0:T(8,128)(2,1)S(1)}, u32[]{:S(2)}, u32[]{:S(2)}) %collective-permute-start.7) | collective-permute-done | bytes 327712 | tf_op jit(solution)/shard_map/ppermute | solution.py:19
  54.7 13.5 %all-to-all-start = ((bf16[64,8,640]{2,1,0:T(8,128)(2,1)}), bf16[64,8,640]{2,1,0:T(8,128)(2,1)S(1)}, u32[]{:S(2)}, u32[]{:S(2)}) async-start(bf16[64,8,640]{2,1,0:T(8,128)(2,1)} %get-tuple-element.48), calls=%async_computation | async-start | bytes 1310720 | tf_op jit(solution)/shard_map/all_to_all | solution.py:374
  68.3 4.4 %collective-permute-start.13 = (bf16[512,512]{1,0:T(8,128)(2,1)S(1)}, bf16[512,512]{1,0:T(8,128)(2,1)S(1)}, u32[]{:S(2)}, u32[]{:S(2)}) collective-permute-start(bf16[512,512]{1,0:T(8,128)(2,1)S(1)} %bitcast.24), channel_id=1, source_target_pairs={{0,2},{1,3},{2,0},{3,1},{4,6},{5,7},{6,4},{7,5},{8,10},{9,11},{10,... | collective-permute-start | bytes 1572872 | tf_op jit(solution)/shard_map/ppermute | solution.py:19
  72.7 2.0 %collective-permute-start.17 = (bf16[128,512]{1,0:T(8,128)(2,1)S(1)}, bf16[128,512]{1,0:T(8,128)(2,1)}, u32[]{:S(2)}, u32[]{:S(2)}) collective-permute-start(bf16[128,512]{1,0:T(8,128)(2,1)S(1)} %bitcast.29), channel_id=1, source_target_pairs={{0,1},{1,2},{2,3},{3,0},{4,5},{5,6},{6,7},{7,4},{8,9},{9,10},{10,1... | collective-permute-start | bytes 393224 | tf_op jit(solution)/shard_map/ppermute | solution.py:19
  74.7 9.9 %collective-permute-done.14.l3 = bf16[512,512]{1,0:T(8,128)(2,1)S(1)} collective-permute-done((bf16[512,512]{1,0:T(8,128)(2,1)S(1)}, bf16[512,512]{1,0:T(8,128)(2,1)S(1)}, u32[]{:S(2)}, u32[]{:S(2)}) %collective-permute-start.14) | collective-permute-done | bytes 524320 | tf_op jit(solution)/shard_map/ppermute | solution.py:19
  86.0 10.7 %collective-permute-done.13.l2 = bf16[512,512]{1,0:T(8,128)(2,1)S(1)} collective-permute-done((bf16[512,512]{1,0:T(8,128)(2,1)S(1)}, bf16[512,512]{1,0:T(8,128)(2,1)S(1)}, u32[]{:S(2)}, u32[]{:S(2)}) %collective-permute-start.13) | collective-permute-done | bytes 524320 | tf_op jit(solution)/shard_map/ppermute | solution.py:19
  96.7 4.8 %second_products.1 = (bf16[512,512]{1,0:T(8,128)(2,1)S(1)}, bf16[512,512]{1,0:T(8,128)(2,1)S(1)}, bf16[512,512]{1,0:T(8,128)(2,1)S(1)}, bf16[512,512]{1,0:T(8,128)(2,1)S(1)}, f32[512,512]{1,0:T(8,128)S(1)}) custom-call(s32[2]{0:T(128)S(1)} %pad_add_fusion.ids, s32[64,4]{1,0:T(8,128)S(1)} %copy.14.anc, s32[64]{0:T(128)S(1)} %copy-done.4, ...), custom_call_target="tpu_custom_call" | custom-call | flops 1610612736 | bytes 9437184 | tf_op jit(solution)/shard_map/second_products/pallas_call | solution.py:207
  104.7 10.5 %all-to-all-start.1 = ((bf16[64,8,640]{2,1,0:T(8,128)(2,1)}), bf16[64,8,640]{2,1,0:T(8,128)(2,1)S(1)}, u32[]{:S(2)}, u32[]{:S(2)}) async-start(bf16[64,8,640]{2,1,0:T(8,128)(2,1)} %pick_parents.1), calls=%async_computation.1 | async-start | bytes 1310720 | tf_op jit(solution)/shard_map/all_to_all | solution.py:382
  115.2 1.6 collective-permute-start.21
  116.7 3.4 %collective-permute-start.22 = (bf16[512,512]{1,0:T(8,128)(2,1)}, bf16[512,512]{1,0:T(8,128)(2,1)}, u32[]{:S(2)}, u32[]{:S(2)}) collective-permute-start(bf16[512,512]{1,0:T(8,128)(2,1)} %copy-done.5), channel_id=1, source_target_pairs={{0,2},{1,3},{2,0},{3,1},{4,6},{5,7},{6,4},{7,5},{8,10},{9,11},{10,... | collective-permute-start | bytes 1572872 | tf_op jit(solution)/shard_map/ppermute | solution.py:19
  120.6 13.8 %all-to-all-done.1.came = bf16[64,8,640]{2,1,0:T(8,128)(2,1)S(1)} async-done(((bf16[64,8,640]{2,1,0:T(8,128)(2,1)}), bf16[64,8,640]{2,1,0:T(8,128)(2,1)S(1)}, u32[]{:S(2)}, u32[]{:S(2)}) %all-to-all-start.1) | async-done | bytes 655392 | tf_op jit(solution)/shard_map/all_to_all | solution.py:382
  134.4 2.7 %last_products.1 = (f32[512,512]{1,0:T(8,128)S(1)}, f32[128,512]{1,0:T(8,128)S(1)}, f32[128,512]{1,0:T(8,128)S(1)}, bf16[128,512]{1,0:T(8,128)(2,1)S(1)}, bf16[1...) custom-call(s32[2]{0:T(128)S(1)} %pad_add_fusion.ids, ...), custom_call_target="tpu_custom_call" | custom-call | flops 1342177280 | bytes 6291456 | tf_op jit(solution)/shard_map/last_products/pallas_call | solution.py:335
  137.2 1.8 %collective-permute-start.18 = (bf16[128,512]{1,0:T(8,128)(2,1)S(1)}, bf16[128,512]{1,0:T(8,128)(2,1)S(1)}, u32[]{:S(2)}, u32[]{:S(2)}) collective-permute-start(bf16[128,512]{1,0:T(8,128)(2,1)S(1)} %get-tuple-element.62), channel_id=1, source_target_pairs={{0,1},{1,2},{2,3},{3,0},{4,5},{5,6},{6,7},{7,4},{8,9},{9,10},{10,1... | collective-permute-start | bytes 393224 | tf_op jit(solution)/shard_map/ppermute | solution.py:19
  139.0 2.0 %collective-permute-start.20 = (bf16[128,512]{1,0:T(8,128)(2,1)S(1)}, bf16[128,512]{1,0:T(8,128)(2,1)S(1)}, u32[]{:S(2)}, u32[]{:S(2)}) collective-permute-start(bf16[128,512]{1,0:T(8,128)(2,1)S(1)} %get-tuple-element.63), channel_id=1, source_target_pairs={{0,3},{1,0},{2,1},{3,2},{4,7},{5,4},{6,5},{7,6},{8,11},{9,8},{10,9... | collective-permute-start | bytes 393224 | tf_op jit(solution)/shard_map/ppermute | solution.py:19
  141.0 5.4 %collective-permute-done.18 = bf16[128,512]{1,0:T(8,128)(2,1)S(1)} collective-permute-done((bf16[128,512]{1,0:T(8,128)(2,1)S(1)}, bf16[128,512]{1,0:T(8,128)(2,1)S(1)}, u32[]{:S(2)}, u32[]{:S(2)}) %collective-permute-start.18) | collective-permute-done | bytes 131104 | tf_op jit(solution)/shard_map/ppermute | solution.py:19
  146.4 3.3 %collective-permute-start.25 = (bf16[128,512]{1,0:T(8,128)(2,1)S(1)}, bf16[128,512]{1,0:T(8,128)(2,1)S(1)}, u32[]{:S(2)}, u32[]{:S(2)}) collective-permute-start(bf16[128,512]{1,0:T(8,128)(2,1)S(1)} %get-tuple-element.72), channel_id=1, source_target_pairs={{0,3},{1,0},{2,1},{3,2},{4,7},{5,4},{6,5},{7,6},{8,11},{9,8},{10,9... | collective-permute-start | bytes 393224 | tf_op jit(solution)/shard_map/ppermute | solution.py:19
  149.7 2.5 %fusion = bf16[1,512,512]{2,1,0:T(8,128)(2,1)} fusion(bf16[512,512]{1,0:T(8,128)(2,1)} %collective-permute-done.23, bf16[512,512]{1,0:T(8,128)(2,1)} %collective-permute-done.22, bf16[512,512]{1,0:T(8,128)(2,1)} %collective-permute-done.21, f32[512,512]{1,0:T(8,128)S(1)} %get-tuple-element.64, bf16[512,512]{1,0:T(8,128)(2,1)S(1)} %get-tuple-element.65), kind=kLoop, calls=%fused_computation.1 | loop fusion | flops 2621440 | bytes 3670016 | tf_op jit(solution)/shard_map/broadcast_in_dim | solution.py:398
  152.5 3.8 %collective-permute-start.26 = (bf16[128,512]{1,0:T(8,128)(2,1)S(1)}, bf16[128,512]{1,0:T(8,128)(2,1)S(1)}, u32[]{:S(2)}, u32[]{:S(2)}) collective-permute-start(bf16[128,512]{1,0:T(8,128)(2,1)S(1)} %add.50), channel_id=1, source_target_pairs={{0,3},{1,0},{2,1},{3,2},{4,7},{5,4},{6,5},{7,6},{8,11},{9,8},{10,9... | collective-permute-start | bytes 393224 | tf_op jit(solution)/shard_map/ppermute | solution.py:19
  156.9 1.8 %collective-permute-done.26 = bf16[128,512]{1,0:T(8,128)(2,1)S(1)} collective-permute-done((bf16[128,512]{1,0:T(8,128)(2,1)S(1)}, bf16[128,512]{1,0:T(8,128)(2,1)S(1)}, u32[]{:S(2)}, u32[]{:S(2)}) %collective-permute-start.26) | collective-permute-done | bytes 131104 | tf_op jit(solution)/shard_map/ppermute | solution.py:19
  158.7 1.6 %fusion.5 = bf16[1,128,512]{2,1,0:T(8,128)(2,1)} fusion(bf16[128,512]{1,0:T(8,128)(2,1)S(1)} %collective-permute-done.26, bf16[128,512]{1,0:T(8,128)(2,1)S(1)} %collective-permute-done.24, f32[128,512]{1,0:T(8,128)S(1)} %get-tuple-element.69, bf16[1,128,512]{2,1,0:T(8,128)(2,1)} %param.15), kind=kLoop, calls=%fused_computation.10 | loop fusion | flops 458752 | bytes 786432 | tf_op jit(solution)/shard_map/broadcast_in_dim | solution.py:399
  (58 shorter events, 12.6 us)
Async XLA Ops:
  1.7 9.8 %collective-permute-start.1 = (bf16[256,512]{1,0:T(8,128)(2,1)S(1)}, bf16[256,512]{1,0:T(8,128)(2,1)S(1)}, u32[]{:S(2)}, u32[]{:S(2)}) collective-permute-start(bf16[256,512]{1,0:T(8,128)(2,1)S(1)} %get-tuple-element.73), channel_id=1, source_target_pairs={{0,3},{1,0},{2,1},{3,2},{4,7},{5,4},{6,5},{7,6},{8,11},{9,8},{10,9... | collective-permute-start | bytes 786440 | tf_op jit(solution)/shard_map/ppermute | solution.py:19
  4.8 10.4 %collective-permute-start.2 = (bf16[256,512]{1,0:T(8,128)(2,1)S(1)}, bf16[256,512]{1,0:T(8,128)(2,1)S(1)}, u32[]{:S(2)}, u32[]{:S(2)}) collective-permute-start(bf16[256,512]{1,0:T(8,128)(2,1)S(1)} %get-tuple-element.74), channel_id=1, source_target_pairs={{0,1},{1,2},{2,3},{3,0},{4,5},{5,6},{6,7},{7,4},{8,9},{9,10},{10,1... | collective-permute-start | bytes 786440 | tf_op jit(solution)/shard_map/ppermute | solution.py:19
  4.8 16.1 %collective-permute-start.5 = (bf16[256,512]{1,0:T(8,128)(2,1)S(1)}, bf16[256,512]{1,0:T(8,128)(2,1)S(1)}, u32[]{:S(2)}, u32[]{:S(2)}) collective-permute-start(bf16[256,512]{1,0:T(8,128)(2,1)S(1)} %get-tuple-element.73), channel_id=1, source_target_pairs={{0,1},{1,2},{2,3},{3,0},{4,5},{5,6},{6,7},{7,4},{8,9},{9,10},{10,1... | collective-permute-start | bytes 786440 | tf_op jit(solution)/shard_map/ppermute | solution.py:19
  5.4 15.5 %collective-permute-start = (bf16[256,512]{1,0:T(8,128)(2,1)S(1)}, bf16[256,512]{1,0:T(8,128)(2,1)S(1)}, u32[]{:S(2)}, u32[]{:S(2)}) collective-permute-start(bf16[256,512]{1,0:T(8,128)(2,1)S(1)} %get-tuple-element.74), channel_id=1, source_target_pairs={{0,3},{1,0},{2,1},{3,2},{4,7},{5,4},{6,5},{7,6},{8,11},{9,8},{10,9... | collective-permute-start | bytes 786440 | tf_op jit(solution)/shard_map/ppermute | solution.py:19
  11.5 15.4 %collective-permute-start.4 = (bf16[256,512]{1,0:T(8,128)(2,1)S(1)}, bf16[256,512]{1,0:T(8,128)(2,1)S(1)}, u32[]{:S(2)}, u32[]{:S(2)}) collective-permute-start(bf16[256,512]{1,0:T(8,128)(2,1)S(1)} %collective-permute-done.1.p1b), channel_id=1, source_target_pairs={{0,3},{1,0},{2,1},{3,2},{4,7},{5,4},{6,5},{7,6},{8,11},{9,8},{10,9... | collective-permute-start | bytes 786440 | tf_op jit(solution)/shard_map/ppermute | solution.py:19
  15.2 11.6 %collective-permute-start.3 = (bf16[256,512]{1,0:T(8,128)(2,1)S(1)}, bf16[256,512]{1,0:T(8,128)(2,1)S(1)}, u32[]{:S(2)}, u32[]{:S(2)}) collective-permute-start(bf16[256,512]{1,0:T(8,128)(2,1)S(1)} %collective-permute-done.2.p3t), channel_id=1, source_target_pairs={{0,1},{1,2},{2,3},{3,0},{4,5},{5,6},{6,7},{7,4},{8,9},{9,10},{10,1... | collective-permute-start | bytes 786440 | tf_op jit(solution)/shard_map/ppermute | solution.py:19
  26.9 41.3 %copy-start.2 = (bf16[1,512,512]{2,1,0:T(8,128)(2,1)S(1)}, bf16[1,512,512]{2,1,0:T(8,128)(2,1)}, u32[]{:S(2)}) copy-start(bf16[1,512,512]{2,1,0:T(8,128)(2,1)} %param.14) | copy-start | bytes 1572868
  26.9 45.8 %copy-start.7 = (bf16[1,128,512]{2,1,0:T(8,128)(2,1)S(1)}, bf16[1,128,512]{2,1,0:T(8,128)(2,1)}, u32[]{:S(2)}) copy-start(bf16[1,128,512]{2,1,0:T(8,128)(2,1)} %param.13) | copy-start | bytes 393220
  26.9 69.9 %copy-start.4 = (s32[64]{0:T(128)S(1)}, s32[64]{0:T(128)}, u32[]{:S(2)}) copy-start(s32[64]{0:T(128)} %parents.3) | copy-start | bytes 772
  30.7 11.9 %collective-permute-start.6 = (bf16[320,512]{1,0:T(8,128)(2,1)S(1)}, bf16[320,512]{1,0:T(8,128)(2,1)S(1)}, u32[]{:S(2)}, u32[]{:S(2)}) collective-permute-start(bf16[320,512]{1,0:T(8,128)(2,1)S(1)} %get-tuple-element.41), channel_id=1, source_target_pairs={{0,1},{1,2},{2,3},{3,0},{4,5},{5,6},{6,7},{7,4},{8,9},{9,10},{10,1... | collective-permute-start | bytes 983048 | tf_op jit(solution)/shard_map/ppermute | solution.py:19
  30.8 12.0 %collective-permute-start.10 = (bf16[320,512]{1,0:T(8,128)(2,1)S(1)}, bf16[320,512]{1,0:T(8,128)(2,1)S(1)}, u32[]{:S(2)}, u32[]{:S(2)}) collective-permute-start(bf16[320,512]{1,0:T(8,128)(2,1)S(1)} %get-tuple-element.45), channel_id=1, source_target_pairs={{0,3},{1,0},{2,1},{3,2},{4,7},{5,4},{6,5},{7,6},{8,11},{9,8},{10,9... | collective-permute-start | bytes 983048 | tf_op jit(solution)/shard_map/ppermute | solution.py:19
  34.1 15.6 %collective-permute-start.8 = (bf16[320,512]{1,0:T(8,128)(2,1)S(1)}, bf16[320,512]{1,0:T(8,128)(2,1)S(1)}, u32[]{:S(2)}, u32[]{:S(2)}) collective-permute-start(bf16[320,512]{1,0:T(8,128)(2,1)S(1)} %get-tuple-element.42), channel_id=1, source_target_pairs={{0,1},{1,2},{2,3},{3,0},{4,5},{5,6},{6,7},{7,4},{8,9},{9,10},{10,1... | collective-permute-start | bytes 983048 | tf_op jit(solution)/shard_map/ppermute | solution.py:19
  34.1 15.6 %collective-permute-start.9 = (bf16[320,512]{1,0:T(8,128)(2,1)S(1)}, bf16[320,512]{1,0:T(8,128)(2,1)S(1)}, u32[]{:S(2)}, u32[]{:S(2)}) collective-permute-start(bf16[320,512]{1,0:T(8,128)(2,1)S(1)} %get-tuple-element.43), channel_id=1, source_target_pairs={{0,3},{1,0},{2,1},{3,2},{4,7},{5,4},{6,5},{7,6},{8,11},{9,8},{10,9... | collective-permute-start | bytes 983048 | tf_op jit(solution)/shard_map/ppermute | solution.py:19
  42.8 10.7 %collective-permute-start.7 = (bf16[320,512]{1,0:T(8,128)(2,1)S(1)}, bf16[320,512]{1,0:T(8,128)(2,1)S(1)}, u32[]{:S(2)}, u32[]{:S(2)}) collective-permute-start(bf16[320,512]{1,0:T(8,128)(2,1)S(1)} %add.39), channel_id=1, source_target_pairs={{0,1},{1,2},{2,3},{3,0},{4,5},{5,6},{6,7},{7,4},{8,9},{9,10},{10,1... | collective-permute-start | bytes 983048 | tf_op jit(solution)/shard_map/ppermute | solution.py:19
  43.0 10.5 %collective-permute-start.11 = (bf16[320,512]{1,0:T(8,128)(2,1)S(1)}, bf16[320,512]{1,0:T(8,128)(2,1)S(1)}, u32[]{:S(2)}, u32[]{:S(2)}) collective-permute-start(bf16[320,512]{1,0:T(8,128)(2,1)S(1)} %add.40), channel_id=1, source_target_pairs={{0,3},{1,0},{2,1},{3,2},{4,7},{5,4},{6,5},{7,6},{8,11},{9,8},{10,9... | collective-permute-start | bytes 983048 | tf_op jit(solution)/shard_map/ppermute | solution.py:19
  54.7 48.5 %all-to-all-start = ((bf16[64,8,640]{2,1,0:T(8,128)(2,1)}), bf16[64,8,640]{2,1,0:T(8,128)(2,1)S(1)}, u32[]{:S(2)}, u32[]{:S(2)}) async-start(bf16[64,8,640]{2,1,0:T(8,128)(2,1)} %get-tuple-element.48), calls=%async_computation | async-start | bytes 1310720 | tf_op jit(solution)/shard_map/all_to_all | solution.py:374
  68.2 16.5 %collective-permute-start.14 = (bf16[512,512]{1,0:T(8,128)(2,1)S(1)}, bf16[512,512]{1,0:T(8,128)(2,1)S(1)}, u32[]{:S(2)}, u32[]{:S(2)}) collective-permute-start(bf16[512,512]{1,0:T(8,128)(2,1)S(1)} %bitcast.23), channel_id=1, source_target_pairs={{0,1},{1,2},{2,3},{3,0},{4,5},{5,6},{6,7},{7,4},{8,9},{9,10},{10,1... | collective-permute-start | bytes 1572872 | tf_op jit(solution)/shard_map/ppermute | solution.py:19
  68.3 28.4 %collective-permute-start.13 = (bf16[512,512]{1,0:T(8,128)(2,1)S(1)}, bf16[512,512]{1,0:T(8,128)(2,1)S(1)}, u32[]{:S(2)}, u32[]{:S(2)}) collective-permute-start(bf16[512,512]{1,0:T(8,128)(2,1)S(1)} %bitcast.24), channel_id=1, source_target_pairs={{0,2},{1,3},{2,0},{3,1},{4,6},{5,7},{6,4},{7,5},{8,10},{9,11},{10,... | collective-permute-start | bytes 1572872 | tf_op jit(solution)/shard_map/ppermute | solution.py:19
  72.7 24.0 %collective-permute-start.12 = (bf16[512,512]{1,0:T(8,128)(2,1)S(1)}, bf16[512,512]{1,0:T(8,128)(2,1)S(1)}, u32[]{:S(2)}, u32[]{:S(2)}) collective-permute-start(bf16[512,512]{1,0:T(8,128)(2,1)S(1)} %bitcast.25), channel_id=1, source_target_pairs={{0,3},{1,0},{2,1},{3,2},{4,7},{5,4},{6,5},{7,6},{8,11},{9,8},{10,9... | collective-permute-start | bytes 1572872 | tf_op jit(solution)/shard_map/ppermute | solution.py:19
  72.7 32.0 %collective-permute-start.17 = (bf16[128,512]{1,0:T(8,128)(2,1)S(1)}, bf16[128,512]{1,0:T(8,128)(2,1)}, u32[]{:S(2)}, u32[]{:S(2)}) collective-permute-start(bf16[128,512]{1,0:T(8,128)(2,1)S(1)} %bitcast.29), channel_id=1, source_target_pairs={{0,1},{1,2},{2,3},{3,0},{4,5},{5,6},{6,7},{7,4},{8,9},{9,10},{10,1... | collective-permute-start | bytes 393224 | tf_op jit(solution)/shard_map/ppermute | solution.py:19
  74.7 30.0 %collective-permute-start.16 = (bf16[128,512]{1,0:T(8,128)(2,1)S(1)}, bf16[128,512]{1,0:T(8,128)(2,1)}, u32[]{:S(2)}, u32[]{:S(2)}) collective-permute-start(bf16[128,512]{1,0:T(8,128)(2,1)S(1)} %bitcast.30), channel_id=1, source_target_pairs={{0,2},{1,3},{2,0},{3,1},{4,6},{5,7},{6,4},{7,5},{8,10},{9,11},{10,... | collective-permute-start | bytes 393224 | tf_op jit(solution)/shard_map/ppermute | solution.py:19
  84.7 20.0 %collective-permute-start.15 = (bf16[128,512]{1,0:T(8,128)(2,1)S(1)}, bf16[128,512]{1,0:T(8,128)(2,1)}, u32[]{:S(2)}, u32[]{:S(2)}) collective-permute-start(bf16[128,512]{1,0:T(8,128)(2,1)S(1)} %bitcast.31), channel_id=1, source_target_pairs={{0,3},{1,0},{2,1},{3,2},{4,7},{5,4},{6,5},{7,6},{8,11},{9,8},{10,9... | collective-permute-start | bytes 393224 | tf_op jit(solution)/shard_map/ppermute | solution.py:19
  104.7 29.8 %all-to-all-start.1 = ((bf16[64,8,640]{2,1,0:T(8,128)(2,1)}), bf16[64,8,640]{2,1,0:T(8,128)(2,1)S(1)}, u32[]{:S(2)}, u32[]{:S(2)}) async-start(bf16[64,8,640]{2,1,0:T(8,128)(2,1)} %pick_parents.1), calls=%async_computation.1 | async-start | bytes 1310720 | tf_op jit(solution)/shard_map/all_to_all | solution.py:382
  115.2 31.2 %collective-permute-start.21 = (bf16[512,512]{1,0:T(8,128)(2,1)}, bf16[512,512]{1,0:T(8,128)(2,1)}, u32[]{:S(2)}, u32[]{:S(2)}) collective-permute-start(bf16[512,512]{1,0:T(8,128)(2,1)} %copy-done.6), channel_id=1, source_target_pairs={{0,1},{1,2},{2,3},{3,0},{4,5},{5,6},{6,7},{7,4},{8,9},{9,10},{10,1... | collective-permute-start | bytes 1572872 | tf_op jit(solution)/shard_map/ppermute | solution.py:19
  116.7 32.9 %collective-permute-start.22 = (bf16[512,512]{1,0:T(8,128)(2,1)}, bf16[512,512]{1,0:T(8,128)(2,1)}, u32[]{:S(2)}, u32[]{:S(2)}) collective-permute-start(bf16[512,512]{1,0:T(8,128)(2,1)} %copy-done.5), channel_id=1, source_target_pairs={{0,2},{1,3},{2,0},{3,1},{4,6},{5,7},{6,4},{7,5},{8,10},{9,11},{10,... | collective-permute-start | bytes 1572872 | tf_op jit(solution)/shard_map/ppermute | solution.py:19
  120.1 29.6 %collective-permute-start.23 = (bf16[512,512]{1,0:T(8,128)(2,1)S(1)}, bf16[512,512]{1,0:T(8,128)(2,1)}, u32[]{:S(2)}, u32[]{:S(2)}) collective-permute-start(bf16[512,512]{1,0:T(8,128)(2,1)S(1)} %get-tuple-element.68), channel_id=1, source_target_pairs={{0,3},{1,0},{2,1},{3,2},{4,7},{5,4},{6,5},{7,6},{8,11},{9,8},{10,9... | collective-permute-start | bytes 1572872 | tf_op jit(solution)/shard_map/ppermute | solution.py:19
  137.2 9.1 %collective-permute-start.18 = (bf16[128,512]{1,0:T(8,128)(2,1)S(1)}, bf16[128,512]{1,0:T(8,128)(2,1)S(1)}, u32[]{:S(2)}, u32[]{:S(2)}) collective-permute-start(bf16[128,512]{1,0:T(8,128)(2,1)S(1)} %get-tuple-element.62), channel_id=1, source_target_pairs={{0,1},{1,2},{2,3},{3,0},{4,5},{5,6},{6,7},{7,4},{8,9},{9,10},{10,1... | collective-permute-start | bytes 393224 | tf_op jit(solution)/shard_map/ppermute | solution.py:19
  139.0 17.3 %collective-permute-start.20 = (bf16[128,512]{1,0:T(8,128)(2,1)S(1)}, bf16[128,512]{1,0:T(8,128)(2,1)S(1)}, u32[]{:S(2)}, u32[]{:S(2)}) collective-permute-start(bf16[128,512]{1,0:T(8,128)(2,1)S(1)} %get-tuple-element.63), channel_id=1, source_target_pairs={{0,3},{1,0},{2,1},{3,2},{4,7},{5,4},{6,5},{7,6},{8,11},{9,8},{10,9... | collective-permute-start | bytes 393224 | tf_op jit(solution)/shard_map/ppermute | solution.py:19
  146.3 10.6 %collective-permute-start.24 = (bf16[128,512]{1,0:T(8,128)(2,1)S(1)}, bf16[128,512]{1,0:T(8,128)(2,1)S(1)}, u32[]{:S(2)}, u32[]{:S(2)}) collective-permute-start(bf16[128,512]{1,0:T(8,128)(2,1)S(1)} %get-tuple-element.70), channel_id=1, source_target_pairs={{0,1},{1,2},{2,3},{3,0},{4,5},{5,6},{6,7},{7,4},{8,9},{9,10},{10,1... | collective-permute-start | bytes 393224 | tf_op jit(solution)/shard_map/ppermute | solution.py:19
  146.4 6.1 %collective-permute-start.25 = (bf16[128,512]{1,0:T(8,128)(2,1)S(1)}, bf16[128,512]{1,0:T(8,128)(2,1)S(1)}, u32[]{:S(2)}, u32[]{:S(2)}) collective-permute-start(bf16[128,512]{1,0:T(8,128)(2,1)S(1)} %get-tuple-element.72), channel_id=1, source_target_pairs={{0,3},{1,0},{2,1},{3,2},{4,7},{5,4},{6,5},{7,6},{8,11},{9,8},{10,9... | collective-permute-start | bytes 393224 | tf_op jit(solution)/shard_map/ppermute | solution.py:19
  149.7 6.6 %collective-permute-start.19 = (bf16[128,512]{1,0:T(8,128)(2,1)S(1)}, bf16[128,512]{1,0:T(8,128)(2,1)S(1)}, u32[]{:S(2)}, u32[]{:S(2)}) collective-permute-start(bf16[128,512]{1,0:T(8,128)(2,1)S(1)} %add.41), channel_id=1, source_target_pairs={{0,1},{1,2},{2,3},{3,0},{4,5},{5,6},{6,7},{7,4},{8,9},{9,10},{10,1... | collective-permute-start | bytes 393224 | tf_op jit(solution)/shard_map/ppermute | solution.py:19
  152.5 6.3 %collective-permute-start.26 = (bf16[128,512]{1,0:T(8,128)(2,1)S(1)}, bf16[128,512]{1,0:T(8,128)(2,1)S(1)}, u32[]{:S(2)}, u32[]{:S(2)}) collective-permute-start(bf16[128,512]{1,0:T(8,128)(2,1)S(1)} %add.50), channel_id=1, source_target_pairs={{0,3},{1,0},{2,1},{3,2},{4,7},{5,4},{6,5},{7,6},{8,11},{9,8},{10,9... | collective-permute-start | bytes 393224 | tf_op jit(solution)/shard_map/ppermute | solution.py:19
  (5 other events, 30.6 us)

commit v2 on v1

v2 whole, which is shorter than its diff:
```python
import functools

import jax
import jax.numpy as jnp
from jax import lax
from jax.experimental import pallas as pl
from jax.experimental.pallas import tpu as pltpu
from jax.sharding import PartitionSpec as P

BF = jnp.bfloat16
F32 = jnp.float32
MIB = 1024 * 1024
VMEM_BYTES = 16 * MIB


def vmem():
    return pl.BlockSpec(memory_space=pltpu.VMEM)


def shift(value, step):
    n = lax.axis_size("rows")
    return lax.ppermute(value, "rows", [(i, (i + step) % n) for i in range(n)])


def rows_dot(lhs, rhs):
    return lax.dot_general(lhs, rhs, (((0,), (0,)), ((), ())), preferred_element_type=F32)


def halves_of(block):
    half = block.shape[0] // 2
    return block[:half], block[half:]


def gather_rows(block, top, bottom):
    left_top = shift(top, 1)
    right_bottom = shift(bottom, -1)
    left_bottom = shift(bottom, 1)
    right_top = shift(top, -1)
    far_top = shift(left_top, 1)
    far_bottom = shift(right_bottom, -1)
    return (block, right_top, right_bottom, far_top, far_bottom, left_top, left_bottom)


def scatter_rows(next_two, before_two, next_a, next_b, before_a, before_b):
    from_left_two = shift(next_two, 1)
    from_right_two = shift(before_two, -1)
    left_b = shift(next_b, 1)
    right_a = shift(before_a, -1)
    left_a = shift(next_a + from_left_two, 1)
    right_b = shift(before_b + from_right_two, -1)
    return left_a, left_b, right_a, right_b


def fetch(root, tiles, sems, hits, columns):
    width = tiles.shape[-1]
    copies = []
    for l in range(tiles.shape[0]):
        for k, column in enumerate(columns):
            start = pl.multiple_of(column * width, width)
            source = root.at[pl.ds(l * width, width), pl.ds(start, width)]
            copies.append(pltpu.make_async_copy(source, tiles.at[l, k], sems.at[l, k]))

    def each(l, act):
        @pl.when(hits[l])
        def _():
            for copy in copies[l * len(columns) : (l + 1) * len(columns)]:
                act(copy)

    for l in range(tiles.shape[0]):
        each(l, lambda copy: copy.start())
    return lambda l: each(l, lambda copy: copy.wait())


def hits_of(anc, node, row, block):
    return [anc[node, lax.rem(row + d, 4)] == 2 * row + block for d in range(4)]


def near_kernel(ids, anc, p0, p1t, p1b, p3t, p3b, root, out, tiles, sems):
    width = p0.shape[0]
    half = width // 2
    node, row = ids[0], ids[1]
    some = [functools.reduce(jnp.logical_or, hits_of(anc, node, row, l)) for l in range(2)]
    ready = fetch(root, tiles, sems, some, [anc[node, lax.rem(row + k, 4)] for k in (0, 1, 3)])
    for l in range(2):
        ready(l)

        @pl.when(some[l])
        def _():
            total = jnp.dot(tiles[l, 0], p0[...], preferred_element_type=F32)
            for k, top, bottom in ((1, p1t, p1b), (2, p3t, p3b)):
                total += jnp.dot(tiles[l, k, :, :half], top[...], preferred_element_type=F32)
                total += jnp.dot(tiles[l, k, :, half:], bottom[...], preferred_element_type=F32)
            out[l * width : (l + 1) * width, :] = total


def first_kernel(ids, anc, p0, p1t, p1b, p2t, p2b, p3t, p3b, near, root,
                 mine, next_a, next_b, two_a, two_b, before_a, before_b, prod, fix, tiles, sems):
    width = p0.shape[0]
    half = width // 2
    cut = next_a.shape[0]
    node, row = ids[0], ids[1]
    halves = ((p0.at[:half], p0.at[half:]), (p1t, p1b), (p2t, p2b), (p3t, p3b))
    targets = ((mine, None), (next_a, next_b), (two_a, two_b), (before_a, before_b))
    hits = [hits_of(anc, node, row, l) for l in range(2)]
    some = [functools.reduce(jnp.logical_or, h) for h in hits]
    ready = fetch(root, tiles, sems, some, [anc[node, lax.rem(row + 2, 4)]])
    fix[...] = jnp.zeros_like(fix)
    for a, b in targets:
        a[...] = jnp.zeros_like(a)
        if b is not None:
            b[...] = jnp.zeros_like(b)
    for l in range(2):
        ready(l)

        @pl.when(some[l])
        def _():
            total = near[l * width : (l + 1) * width, :]
            total += jnp.dot(tiles[l, 0, :, :half], p2t[...], preferred_element_type=F32)
            total += jnp.dot(tiles[l, 0, :, half:], p2b[...], preferred_element_type=F32)
            prod[...] = (-total).astype(BF)

        for d in range(4):
            a, b = targets[d]
            top, bottom = halves[d]

            @pl.when(hits[l][d])
            def _():
                if b is None:
                    a[:width, :] = prod[...]
                else:
                    a[...] = prod[:cut, :]
                    b[: width - cut, :] = prod[cut:, :]
                fix[...] -= rows_dot(top[...], prod[:half, :])
                fix[...] -= rows_dot(bottom[...], prod[half:, :])

    share = width // 4
    for d in range(4):
        start = pl.multiple_of(lax.rem(row + d, 4) * share, share)
        part = fix[pl.ds(start, share), :].astype(BF)
        a, b = targets[d]
        if b is None:
            a[width:, :] = part
        else:
            b[width - cut :, :] = part


def smem():
    return pl.BlockSpec(memory_space=pltpu.SMEM)


def hbm():
    return pl.BlockSpec(memory_space=pltpu.HBM)


def tile_scratch(width, count):
    return [pltpu.VMEM((2, count, width, width), BF), pltpu.SemaphoreType.DMA((2, count))]


def near_products(ids, ancestors, pieces, root_rows):
    width = pieces[0].shape[0]
    return pl.pallas_call(
        near_kernel,
        out_shape=jax.ShapeDtypeStruct((2 * width, width), F32),
        in_specs=[smem()] * 2 + [vmem()] * len(pieces) + [hbm()],
        out_specs=vmem(),
        scratch_shapes=tile_scratch(width, 3),
        compiler_params=pltpu.CompilerParams(vmem_limit_bytes=50 * MIB),
        cost_estimate=pl.CostEstimate(
            flops=6 * width**3 * 2, bytes_accessed=6 << 20, transcendentals=0
        ),
        name="near_products",
    )(ids, ancestors, *pieces, root_rows)


def first_products(ids, ancestors, pieces, root_rows, near):
    width = pieces[0].shape[0]
    share = width // 4
    cut = (width + share) // 2
    shapes = [(width + share, width)] + [(cut, width)] * 6
    return pl.pallas_call(
        first_kernel,
        out_shape=[jax.ShapeDtypeStruct(s, BF) for s in shapes],
        in_specs=[smem()] * 2 + [vmem()] * (len(pieces) + 1) + [hbm()],
        out_specs=[vmem()] * 7,
        scratch_shapes=[pltpu.VMEM((width, width), BF), pltpu.VMEM((width, width), F32)]
        + tile_scratch(width, 1),
        compiler_params=pltpu.CompilerParams(vmem_limit_bytes=VMEM_BYTES),
        cost_estimate=pl.CostEstimate(
            flops=4 * width**3 * 2, bytes_accessed=8 << 20, transcendentals=0
        ),
        name="first_products",
    )(ids, ancestors, *pieces, near, root_rows)


def second_kernel(ids, anc, parents, l0, l1, l2, l3, root,
                  mine, next_a, next_b, two_a, two_b, before_a, before_b, corr, prod, tiles, sems):
    width = l0.shape[0]
    half = width // 2
    row = ids[1]
    node = parents[ids[0]]
    lows = (l0, l1, l2, l3)
    outs = (
        (mine.at[:half], mine.at[half:]), (next_a, next_b), (two_a, two_b), (before_a, before_b)
    )
    hits = [hits_of(anc, node, row, l) for l in range(2)]
    some = [functools.reduce(jnp.logical_or, h) for h in hits]
    ready = fetch(root, tiles, sems, some, [anc[node, lax.rem(row + k, 4)] for k in range(4)])
    corr[...] = jnp.zeros_like(corr)
    for pair in outs:
        for part in pair:
            part[...] = jnp.zeros_like(part)
    for l in range(2):
        ready(l)

        @pl.when(some[l])
        def _():
            total = jnp.dot(tiles[l, 0], l0[...], preferred_element_type=F32)
            for k in range(1, 4):
                total += jnp.dot(tiles[l, k], lows[k][...], preferred_element_type=F32)
            prod[...] = total.astype(BF)

        for d in range(4):

            @pl.when(hits[l][d])
            def _():
                for k in range(2):
                    outs[d][k][...] = prod[k * half : (k + 1) * half, :]
                corr[...] += rows_dot(lows[d][...], prod[...])


def second_products(ids, ancestors, parents, lows, root_rows):
    width = lows[0].shape[1]
    square, half = (width, width), (width // 2, width)
    return pl.pallas_call(
        second_kernel,
        out_shape=[jax.ShapeDtypeStruct(square, BF)]
        + [jax.ShapeDtypeStruct(half, BF)] * 6
        + [jax.ShapeDtypeStruct(square, F32)],
        in_specs=[smem()] * 3 + [vmem()] * 4 + [hbm()],
        out_specs=[vmem()] * 8,
        scratch_shapes=[pltpu.VMEM(square, BF)] + tile_scratch(width, 4),
        compiler_params=pltpu.CompilerParams(vmem_limit_bytes=46 * MIB),
        cost_estimate=pl.CostEstimate(
            flops=30 * width**3 * 2, bytes_accessed=9 << 20, transcendentals=0
        ),
        name="second_products",
    )(ids, ancestors, parents, *lows, root_rows)


def settle_kernel(mine, left_a, left_b, right_a, right_b, inverse, off, diag, slices):
    width = off.shape[1]
    share = diag.shape[0]
    cut = left_a.shape[0]
    rest = width - cut
    nodes, deep, _ = slices.shape

    def total(m, x, y):
        return m.astype(F32) + x.astype(F32) + y.astype(F32)

    upper = total(mine[:cut, :], left_a[...], right_a[...])
    lower = total(mine[cut:width, :], left_b[:rest, :], right_b[:rest, :])
    off[:cut, :] = upper.astype(BF)
    off[cut:, :] = lower.astype(BF)
    value = inverse[...].astype(F32) + total(mine[width:, :], left_b[rest:, :], right_b[rest:, :])
    diag[...] = value.astype(BF)
    edge = cut // deep
    slices[:edge, :, :width] = upper.reshape(edge, deep, width).astype(BF)
    slices[edge:, :, :width] = lower.reshape(nodes - edge, deep, width).astype(BF)
    groups = share // deep
    for c in range(nodes // groups):
        part = value[:, c * 128 : (c + 1) * 128].reshape(groups, deep, 128)
        slices[c * groups : (c + 1) * groups, :, width:] = part.astype(BF)


def settle(mine, received, inverse, nodes):
    width = inverse.shape[1]
    share = inverse.shape[0]
    deep = width // nodes
    return pl.pallas_call(
        settle_kernel,
        out_shape=(
            jax.ShapeDtypeStruct((width, width), BF),
            jax.ShapeDtypeStruct((share, width), BF),
            jax.ShapeDtypeStruct((nodes, deep, width + share), BF),
        ),
        in_specs=[vmem()] * 6,
        out_specs=(vmem(),) * 3,
        compiler_params=pltpu.CompilerParams(vmem_limit_bytes=VMEM_BYTES),
        cost_estimate=pl.CostEstimate(flops=1 << 21, bytes_accessed=4 << 20, transcendentals=0),
        name="settle_first",
    )(mine, *received, inverse)


def pick_kernel(parents, held, onward):
    def step(i, carry):
        onward[i] = held[parents[i]]
        return carry

    lax.fori_loop(0, onward.shape[0], step, 0, unroll=8)


def pick(parents, held):
    return pl.pallas_call(
        pick_kernel,
        out_shape=jax.ShapeDtypeStruct(held.shape, held.dtype),
        in_specs=[pl.BlockSpec(memory_space=pltpu.SMEM), vmem()],
        out_specs=vmem(),
        compiler_params=pltpu.CompilerParams(vmem_limit_bytes=VMEM_BYTES),
        cost_estimate=pl.CostEstimate(flops=1 << 20, bytes_accessed=2 << 20, transcendentals=0),
        name="pick_parents",
    )(parents, held)


def sum_kernel(own, left_a, left_b, right_a, right_b, out):
    half = left_a.shape[0]
    for rows, left, right in ((slice(0, half), left_a, right_a), (slice(half, None), left_b, right_b)):
        out[rows, :] = own[rows, :].astype(F32) + left[...].astype(F32) + right[...].astype(F32)


def sum_roots(own, received):
    shape = own.shape
    return pl.pallas_call(
        sum_kernel,
        out_shape=jax.ShapeDtypeStruct(shape, F32),
        in_specs=[vmem()] * 5,
        out_specs=vmem(),
        compiler_params=pltpu.CompilerParams(vmem_limit_bytes=VMEM_BYTES),
        cost_estimate=pl.CostEstimate(
            flops=48 * shape[0] ** 3 * 2, bytes_accessed=3 << 20, transcendentals=0
        ),
        name="sum_roots",
    )(own, *received)


def last_kernel(ids, came, u0, u1, u2, u3, low, corr_in, root, off_low, keep_up, keep_diag,
                next_a, next_b, two_a, two_b, before_a, before_b, cross, corr, whole):
    nodes, deep, wide = came.shape
    width = low.shape[1]
    share = wide - width
    row = ids[1]
    for d, part in enumerate((u0, u1, u2, u3)):
        whole[lax.rem(row + d, 4)] = part[...]
    upper = whole[...].reshape(width, width)
    parent_off = came[:, :, :width].astype(F32).reshape(nodes * deep, width).astype(BF)
    groups = share // deep
    parent_diag = jnp.concatenate(
        [
            came[c * groups : (c + 1) * groups, :, width:].astype(F32).reshape(share, 128)
            for c in range(nodes // groups)
        ],
        axis=1,
    ).astype(BF)
    across = rows_dot(parent_off, low[...])
    cross[...] = across
    own = jnp.dot(parent_diag, upper, preferred_element_type=F32)
    lower = jnp.dot(parent_off, upper, preferred_element_type=F32)
    off_low[...] = -(lower + root[...]).astype(BF)
    corr[...] = (
        corr_in[...]
        + rows_dot(u0[...], own.astype(BF))
        + rows_dot(low[...], lower.astype(BF))
        + rows_dot(upper, across.astype(BF))
    )

    def rows_of(ref, d):
        start = pl.multiple_of(lax.rem(row + d, 4) * share, share)
        return ref[pl.ds(start, share), :]

    keep_up[...] = own + rows_of(cross, 0)
    keep_diag[...] = rows_of(corr, 0)
    for d, (a, b) in ((1, (next_a, next_b)), (2, (two_a, two_b)), (3, (before_a, before_b))):
        a[...] = rows_of(cross, d).astype(BF)
        b[...] = rows_of(corr, d).astype(BF)


def last_products(ids, came, ups, low, corr, root):
    width = low.shape[1]
    share = ups[0].shape[0]
    small = jax.ShapeDtypeStruct((share, width), BF)
    kept = jax.ShapeDtypeStruct((share, width), F32)
    return pl.pallas_call(
        last_kernel,
        out_shape=(jax.ShapeDtypeStruct((width, width), BF), kept, kept) + (small,) * 6,
        in_specs=[pl.BlockSpec(memory_space=pltpu.SMEM)] + [vmem()] * 8,
        out_specs=(vmem(),) * 9,
        scratch_shapes=[
            pltpu.VMEM((width, width), F32),
            pltpu.VMEM((width, width), F32),
            pltpu.VMEM((4, share, width), BF),
        ],
        compiler_params=pltpu.CompilerParams(vmem_limit_bytes=VMEM_BYTES),
        cost_estimate=pl.CostEstimate(
            flops=5 * width**3 * 2, bytes_accessed=6 << 20, transcendentals=0
        ),
        name="last_products",
    )(ids, came, *ups, low, corr, root)


def after(value, *others):
    return lax.optimization_barrier((value, *others))[0]


def spread_rows(block):
    return block, shift(block, -1), shift(block, 2), shift(block, 1)


def on_device(root_rows, ancestors, parents, panel_first, inverse_first, panel_upper, panel_lower,
              inverse_second):
    nodes = lax.axis_size("snode")
    ids = jnp.stack([lax.axis_index("snode"), lax.axis_index("rows")]).astype(jnp.int32)
    pieces = gather_rows(panel_first[0], *halves_of(panel_first[0]))
    near = near_products(ids, ancestors, pieces[:3] + pieces[5:], root_rows)
    mine, next_a, next_b, two_a, two_b, before_a, before_b = first_products(
        ids, ancestors, pieces, root_rows, near
    )
    received = scatter_rows(two_a, two_b, next_a, next_b, before_a, before_b)
    off_first, diag_first, slices = settle(mine, received, inverse_first[0], nodes)
    low = panel_lower[0]
    sent, up = lax.optimization_barrier((low, panel_upper[0], off_first))[:2]
    lows, ups = spread_rows(sent), spread_rows(up)
    spread = lax.all_to_all(slices, "snode", split_axis=0, concat_axis=0, tiled=True)
    own, next_a, next_b, two_a, two_b, before_a, before_b, corr = second_products(
        ids, ancestors, parents, lows, root_rows
    )
    picked, ups = lax.optimization_barrier((pick(parents, spread), ups))
    received = scatter_rows(two_a, two_b, next_a, next_b, before_a, before_b)
    came = lax.all_to_all(picked, "snode", split_axis=0, concat_axis=0, tiled=True)
    off_low, keep_up, keep_diag, next_a, next_b, two_a, two_b, before_a, before_b = last_products(
        ids, came, ups, low, corr, sum_roots(own, received)
    )
    left_a, left_b, right_a, right_b = scatter_rows(two_a, two_b, next_a, next_b, before_a, before_b)
    off_up = -(keep_up + left_a.astype(F32) + right_a.astype(F32))
    diag_second = (
        inverse_second[0].astype(F32) + keep_diag + left_b.astype(F32) + right_b.astype(F32)
    )
    return (
        off_first[None],
        diag_first[None],
        off_up.astype(BF)[None],
        off_low[None],
        diag_second.astype(BF)[None],
    )


def solution(mesh):
    split = P("snode", "rows", None)
    return jax.shard_map(
        on_device,
        mesh=mesh,
        in_specs=(P("rows", None), P(), P(), split, split, split, split, split),
        out_specs=(split,) * 5,
        check_vma=False,
    )
```

time: 162 us -> 164 us (1.012)
  waiting for transfers between devices: 62.5 us -> 71.1 us
  starting transfers between devices: 68.3 us -> 65.2 us
  other arithmetic: 5.19 us -> 2.59 us
    ppermute x27 -> x30, waiting for transfers between devices: 48.7 us -> 54.1 us  [shift(): return lax.ppermute(value, 'rows', [(i, (i + step) % n) for i in range(n)])]
    all_to_all x1, waiting for transfers between devices: 13.8 us -> 17 us  [on_device(): lax.all_to_all(picked, 'snode', split_axis=0, concat_axis=0, tiled=True)]
    ppermute x27 -> x30, starting transfers between devices: 44.3 us -> 41.6 us  [shift(): return lax.ppermute(value, 'rows', [(i, (i + step) % n) for i in range(n)])]
    broadcast_in_dim x1 -> x0, other arithmetic: 2.54 us -> none  [on_device(): (-off_low).astype(BF)[None]]
    all_to_all x1, starting transfers between devices: 13.5 us -> 11.2 us  [on_device(): lax.all_to_all(slices, 'snode', split_axis=0, concat_axis=0, tiled=True)]
    all_to_all x1, starting transfers between devices: 10.5 us -> 12.4 us  [on_device(): lax.all_to_all(picked, 'snode', split_axis=0, concat_axis=0, tiled=True)]
    unnamed x17 -> x25, local copies, waits for them, and re-layouts: 4.78 us -> 6.32 us
    pallas_call x1 -> x2, Pallas kernels: 3.86 us -> 2.65 us  [the longest x1 2.48 us: first_products(): pl.pallas_call(first_kernel, out_shape=[jax.ShapeDtypeStruct(s, BF) for s...]
  transfers between devices with their start and end apart: 29 -> 32, of which waited for: 11 -> 17; matrix products, arithmetic and copies ran while one was open for 3% -> 2% of each run, Pallas kernels for 8% -> 6%
where the time goes in v2:
time: 164 us; the launch traced here: 163 us
  waiting for transfers between devices  71.1 us (43%)
  starting transfers between devices  65.2 us (40%)
  Pallas kernels  16.2 us (10%)
  local copies, waits for them, and re-layouts  7.39 us (5%)
  other arithmetic  2.59 us (2%)
    ppermute x30, waiting for transfers between devices, shift(): return lax.ppermute(value, 'rows', [(i, (i + step) % n) for i in range(n)])  54.1 us
    ppermute x30, starting transfers between devices, shift(): return lax.ppermute(value, 'rows', [(i, (i + step) % n) for i in range(n)])  41.6 us
    all_to_all x1, waiting for transfers between devices, on_device(): lax.all_to_all(picked, 'snode', split_axis=0, concat_axis=0, tiled=True)  17 us
    all_to_all x1, starting transfers between devices, on_device(): lax.all_to_all(picked, 'snode', split_axis=0, concat_axis=0, tiled=True)  12.4 us
    all_to_all x1, starting transfers between devices, on_device(): lax.all_to_all(slices, 'snode', split_axis=0, concat_axis=0, tiled=True)  11.2 us
    unnamed x25, local copies, waits for them, and re-layouts  6.32 us
    pallas_call x1, Pallas kernels, second_products(): pl.pallas_call(second_kernel, out_shape=[jax.ShapeDtypeStruct(square, BF)...  4.66 us
    pallas_call x1, Pallas kernels, near_products(): pl.pallas_call(near_kernel, out_shape=jax.ShapeDtypeStruct((2 * width, wi...  3.49 us
  transfers between devices with their start and end apart: 32, of which 17 were waited for; matrix products, arithmetic and copies ran while one was open for 2% of the time, Pallas kernels for 6%

profile of v2, /device:TPU:6, one launch (start us, length us, event | category | flops | bytes accessed | tf_op | source)
XLA Modules:
  0.0 163.3 jit_solution(8541569474189209371)
XLA Ops:
  1.7 1.7 %collective-permute-start.2 = (bf16[256,512]{1,0:T(8,128)(2,1)S(1)}, bf16[256,512]{1,0:T(8,128)(2,1)S(1)}, u32[]{:S(2)}, u32[]{:S(2)}) collective-permute-start(bf16[256,512]{1,0:T(8,128)(2,1)S(1)} %get-tuple-element.74), channel_id=1, source_target_pairs={{0,1},{1,2},{2,3},{3,0},{4,5},{5,6},{6,7},{7,4},{8,9},{9,10},{10,1... | collective-permute-start | bytes 786440 | tf_op jit(solution)/shard_map/ppermute | solution.py:22
  3.4 1.7 %collective-permute-start.1 = (bf16[256,512]{1,0:T(8,128)(2,1)S(1)}, bf16[256,512]{1,0:T(8,128)(2,1)S(1)}, u32[]{:S(2)}, u32[]{:S(2)}) collective-permute-start(bf16[256,512]{1,0:T(8,128)(2,1)S(1)} %get-tuple-element.73), channel_id=1, source_target_pairs={{0,3},{1,0},{2,1},{3,2},{4,7},{5,4},{6,5},{7,6},{8,11},{9,8},{10,9... | collective-permute-start | bytes 786440 | tf_op jit(solution)/shard_map/ppermute | solution.py:22
  5.0 1.8 %collective-permute-start = (bf16[256,512]{1,0:T(8,128)(2,1)S(1)}, bf16[256,512]{1,0:T(8,128)(2,1)S(1)}, u32[]{:S(2)}, u32[]{:S(2)}) collective-permute-start(bf16[256,512]{1,0:T(8,128)(2,1)S(1)} %get-tuple-element.74), channel_id=1, source_target_pairs={{0,3},{1,0},{2,1},{3,2},{4,7},{5,4},{6,5},{7,6},{8,11},{9,8},{10,9... | collective-permute-start | bytes 786440 | tf_op jit(solution)/shard_map/ppermute | solution.py:22
  7.8 4.4 %collective-permute-done.2.p3t = bf16[256,512]{1,0:T(8,128)(2,1)S(1)} collective-permute-done((bf16[256,512]{1,0:T(8,128)(2,1)S(1)}, bf16[256,512]{1,0:T(8,128)(2,1)S(1)}, u32[]{:S(2)}, u32[]{:S(2)}) %collective-permute-start.2) | collective-permute-done | bytes 262176 | tf_op jit(solution)/shard_map/ppermute | solution.py:22
  12.6 2.8 %collective-permute-start.4 = (bf16[256,512]{1,0:T(8,128)(2,1)S(1)}, bf16[256,512]{1,0:T(8,128)(2,1)S(1)}, u32[]{:S(2)}, u32[]{:S(2)}) collective-permute-start(bf16[256,512]{1,0:T(8,128)(2,1)S(1)} %collective-permute-done.1.p1b), channel_id=1, source_target_pairs={{0,3},{1,0},{2,1},{3,2},{4,7},{5,4},{6,5},{7,6},{8,11},{9,8},{10,9... | collective-permute-start | bytes 786440 | tf_op jit(solution)/shard_map/ppermute | solution.py:22
  15.5 2.7 %collective-permute-done.p1t = bf16[256,512]{1,0:T(8,128)(2,1)S(1)} collective-permute-done((bf16[256,512]{1,0:T(8,128)(2,1)S(1)}, bf16[256,512]{1,0:T(8,128)(2,1)S(1)}, u32[]{:S(2)}, u32[]{:S(2)}) %collective-permute-start) | collective-permute-done | bytes 262176 | tf_op jit(solution)/shard_map/ppermute | solution.py:22
  19.3 3.5 %near_products.1.near = f32[1024,512]{1,0:T(8,128)S(1)} custom-call(s32[2]{0:T(128)S(1)} %pad_add_fusion.ids, s32[64,4]{1,0:T(8,128)S(1)} %copy.14.anc, bf16[512,512]{1,0:T(8,128)(2,1)S(1)} %bitcast.20, bf16[256,512]{1,0:T(8,128)(2,1)S(1)} %collective-permute-done.p1t, bf16[256,512]{1,0:T(8,128)(2,1)S(1)} %collective-permute-done.1.p1b, ...), custom_call_target="tpu_custom_call" | custom-call | flops 1610612736 | bytes 6291456 | tf_op jit(solution)/shard_map/near_products/pallas_call | solution.py:161
  22.8 2.5 %first_products.1 = (bf16[640,512]{1,0:T(8,128)(2,1)S(1)}, bf16[320,512]{1,0:T(8,128)(2,1)S(1)}, bf16[320,512]{1,0:T(8,128)(2,1)S(1)}, bf16[320,512]{1,0:T(8,128...) custom-call(s32[2]{0:T(128)S(1)} %pad_add_fusion.ids, ...), custom_call_target="tpu_custom_call" | custom-call | flops 1073741824 | bytes 8388608 | tf_op jit(solution)/shard_map/first_products/pallas_call | solution.py:180
  25.3 4.9 %collective-permute-start.10 = (bf16[320,512]{1,0:T(8,128)(2,1)S(1)}, bf16[320,512]{1,0:T(8,128)(2,1)S(1)}, u32[]{:S(2)}, u32[]{:S(2)}) collective-permute-start(bf16[320,512]{1,0:T(8,128)(2,1)S(1)} %get-tuple-element.45), channel_id=1, source_target_pairs={{0,3},{1,0},{2,1},{3,2},{4,7},{5,4},{6,5},{7,6},{8,11},{9,8},{10,9... | collective-permute-start | bytes 983048 | tf_op jit(solution)/shard_map/ppermute | solution.py:22
  30.2 3.3 %collective-permute-start.9 = (bf16[320,512]{1,0:T(8,128)(2,1)S(1)}, bf16[320,512]{1,0:T(8,128)(2,1)S(1)}, u32[]{:S(2)}, u32[]{:S(2)}) collective-permute-start(bf16[320,512]{1,0:T(8,128)(2,1)S(1)} %get-tuple-element.43), channel_id=1, source_target_pairs={{0,3},{1,0},{2,1},{3,2},{4,7},{5,4},{6,5},{7,6},{8,11},{9,8},{10,9... | collective-permute-start | bytes 983048 | tf_op jit(solution)/shard_map/ppermute | solution.py:22
  33.5 4.9 %collective-permute-done.10 = bf16[320,512]{1,0:T(8,128)(2,1)S(1)} collective-permute-done((bf16[320,512]{1,0:T(8,128)(2,1)S(1)}, bf16[320,512]{1,0:T(8,128)(2,1)S(1)}, u32[]{:S(2)}, u32[]{:S(2)}) %collective-permute-start.10) | collective-permute-done | bytes 327712 | tf_op jit(solution)/shard_map/ppermute | solution.py:22
  38.4 3.8 %collective-permute-start.11 = (bf16[320,512]{1,0:T(8,128)(2,1)S(1)}, bf16[320,512]{1,0:T(8,128)(2,1)S(1)}, u32[]{:S(2)}, u32[]{:S(2)}) collective-permute-start(bf16[320,512]{1,0:T(8,128)(2,1)S(1)} %add.34), channel_id=1, source_target_pairs={{0,3},{1,0},{2,1},{3,2},{4,7},{5,4},{6,5},{7,6},{8,11},{9,8},{10,9... | collective-permute-start | bytes 983048 | tf_op jit(solution)/shard_map/ppermute | solution.py:22
  42.4 6.4 %collective-permute-done.8.left_b = bf16[320,512]{1,0:T(8,128)(2,1)S(1)} collective-permute-done((bf16[320,512]{1,0:T(8,128)(2,1)S(1)}, bf16[320,512]{1,0:T(8,128)(2,1)S(1)}, u32[]{:S(2)}, u32[]{:S(2)}) %collective-permute-start.8) | collective-permute-done | bytes 327712 | tf_op jit(solution)/shard_map/ppermute | solution.py:22
  48.9 3.4 %collective-permute-done.7.left_a = bf16[320,512]{1,0:T(8,128)(2,1)S(1)} collective-permute-done((bf16[320,512]{1,0:T(8,128)(2,1)S(1)}, bf16[320,512]{1,0:T(8,128)(2,1)S(1)}, u32[]{:S(2)}, u32[]{:S(2)}) %collective-permute-start.7) | collective-permute-done | bytes 327712 | tf_op jit(solution)/shard_map/ppermute | solution.py:22
  55.6 11.2 %all-to-all-start = ((bf16[64,8,640]{2,1,0:T(8,128)(2,1)}), bf16[64,8,640]{2,1,0:T(8,128)(2,1)S(1)}, u32[]{:S(2)}, u32[]{:S(2)}) async-start(bf16[64,8,640]{2,1,0:T(8,128)(2,1)} %get-tuple-element.48), calls=%async_computation | async-start | bytes 1310720 | tf_op jit(solution)/shard_map/all_to_all | solution.py:421
  66.8 1.6 %collective-permute-done.15.l1 = bf16[512,512]{1,0:T(8,128)(2,1)S(1)} collective-permute-done((bf16[512,512]{1,0:T(8,128)(2,1)S(1)}, bf16[512,512]{1,0:T(8,128)(2,1)S(1)}, u32[]{:S(2)}, u32[]{:S(2)}) %collective-permute-start.15) | collective-permute-done | bytes 524320 | tf_op jit(solution)/shard_map/ppermute | solution.py:22
  68.4 1.8 %collective-permute-done.16.l2 = bf16[512,512]{1,0:T(8,128)(2,1)S(1)} collective-permute-done((bf16[512,512]{1,0:T(8,128)(2,1)S(1)}, bf16[512,512]{1,0:T(8,128)(2,1)S(1)}, u32[]{:S(2)}, u32[]{:S(2)}) %collective-permute-start.16) | collective-permute-done | bytes 524320 | tf_op jit(solution)/shard_map/ppermute | solution.py:22
  70.2 6.5 %collective-permute-done.17.l3 = bf16[512,512]{1,0:T(8,128)(2,1)S(1)} collective-permute-done((bf16[512,512]{1,0:T(8,128)(2,1)S(1)}, bf16[512,512]{1,0:T(8,128)(2,1)S(1)}, u32[]{:S(2)}, u32[]{:S(2)}) %collective-permute-start.17) | collective-permute-done | bytes 524320 | tf_op jit(solution)/shard_map/ppermute | solution.py:22
  76.7 4.7 %second_products.1 = (bf16[512,512]{1,0:T(8,128)(2,1)S(1)}, bf16[256,512]{1,0:T(8,128)(2,1)S(1)}, bf16[256,512]{1,0:T(8,128)(2,1)S(1)}, bf16[256,512]{1,0:T(8,12...) custom-call(s32[2]{0:T(128)S(1)} %pad_add_fusion.ids, ...), custom_call_target="tpu_custom_call" | custom-call | flops 8053063680 | bytes 9437184 | tf_op jit(solution)/shard_map/second_products/pallas_call | solution.py:234
  81.5 2.0 %collective-permute-start.18 = (bf16[256,512]{1,0:T(8,128)(2,1)S(1)}, bf16[256,512]{1,0:T(8,128)(2,1)S(1)}, u32[]{:S(2)}, u32[]{:S(2)}) collective-permute-start(bf16[256,512]{1,0:T(8,128)(2,1)S(1)} %get-tuple-element.59), channel_id=1, source_target_pairs={{0,1},{1,2},{2,3},{3,0},{4,5},{5,6},{6,7},{7,4},{8,9},{9,10},{10,1... | collective-permute-start | bytes 786440 | tf_op jit(solution)/shard_map/ppermute | solution.py:22
  87.5 2.9 %collective-permute-done.22 = bf16[256,512]{1,0:T(8,128)(2,1)S(1)} collective-permute-done((bf16[256,512]{1,0:T(8,128)(2,1)S(1)}, bf16[256,512]{1,0:T(8,128)(2,1)S(1)}, u32[]{:S(2)}, u32[]{:S(2)}) %collective-permute-start.22) | collective-permute-done | bytes 262176 | tf_op jit(solution)/shard_map/ppermute | solution.py:22
  90.5 2.0 %collective-permute-start.21 = (bf16[256,512]{1,0:T(8,128)(2,1)S(1)}, bf16[256,512]{1,0:T(8,128)(2,1)S(1)}, u32[]{:S(2)}, u32[]{:S(2)}) collective-permute-start(bf16[256,512]{1,0:T(8,128)(2,1)S(1)} %get-tuple-element.61), channel_id=1, source_target_pairs={{0,3},{1,0},{2,1},{3,2},{4,7},{5,4},{6,5},{7,6},{8,11},{9,8},{10,9... | collective-permute-start | bytes 786440 | tf_op jit(solution)/shard_map/ppermute | solution.py:22
  96.1 2.2 %collective-permute-start.14 = (bf16[128,512]{1,0:T(8,128)(2,1)}, bf16[128,512]{1,0:T(8,128)(2,1)S(1)}, u32[]{:S(2)}, u32[]{:S(2)}) collective-permute-start(bf16[128,512]{1,0:T(8,128)(2,1)} %bitcast.9.u0), channel_id=1, source_target_pairs={{0,1},{1,2},{2,3},{3,0},{4,5},{5,6},{6,7},{7,4},{8,9},{9,10},{10,1... | collective-permute-start | bytes 393224 | tf_op jit(solution)/shard_map/ppermute | solution.py:22
  98.3 1.5 pick_parents.1
  99.8 9.0 %collective-permute-done.14.u3 = bf16[128,512]{1,0:T(8,128)(2,1)S(1)} collective-permute-done((bf16[128,512]{1,0:T(8,128)(2,1)}, bf16[128,512]{1,0:T(8,128)(2,1)S(1)}, u32[]{:S(2)}, u32[]{:S(2)}) %collective-permute-start.14) | collective-permute-done | bytes 131104 | tf_op jit(solution)/shard_map/ppermute | solution.py:22
  108.8 12.4 %all-to-all-start.1 = ((bf16[64,8,640]{2,1,0:T(8,128)(2,1)}), bf16[64,8,640]{2,1,0:T(8,128)(2,1)S(1)}, u32[]{:S(2)}, u32[]{:S(2)}) async-start(bf16[64,8,640]{2,1,0:T(8,128)(2,1)} %pick_parents.1), calls=%async_computation.1 | async-start | bytes 1310720 | tf_op jit(solution)/shard_map/all_to_all | solution.py:427
  123.5 17.0 %all-to-all-done.1.came = bf16[64,8,640]{2,1,0:T(8,128)(2,1)S(1)} async-done(((bf16[64,8,640]{2,1,0:T(8,128)(2,1)}), bf16[64,8,640]{2,1,0:T(8,128)(2,1)S(1)}, u32[]{:S(2)}, u32[]{:S(2)}) %all-to-all-start.1) | async-done | bytes 655392 | tf_op jit(solution)/shard_map/all_to_all | solution.py:427
  142.9 2.6 %last_products.1 = (bf16[512,512]{1,0:T(8,128)(2,1)}, f32[128,512]{1,0:T(8,128)S(1)}, f32[128,512]{1,0:T(8,128)S(1)}, bf16[128,512]{1,0:T(8,128)(2,1)S(1)}, bf16...) custom-call(s32[2]{0:T(128)S(1)} %pad_add_fusion.ids, ...), custom_call_target="tpu_custom_call" | custom-call | flops 1342177280 | bytes 6291456 | tf_op jit(solution)/shard_map/last_products/pallas_call | solution.py:381
  145.9 3.0 %collective-permute-start.28 = (bf16[128,512]{1,0:T(8,128)(2,1)S(1)}, bf16[128,512]{1,0:T(8,128)(2,1)S(1)}, u32[]{:S(2)}, u32[]{:S(2)}) collective-permute-start(bf16[128,512]{1,0:T(8,128)(2,1)S(1)} %get-tuple-element.72), channel_id=1, source_target_pairs={{0,3},{1,0},{2,1},{3,2},{4,7},{5,4},{6,5},{7,6},{8,11},{9,8},{10,9... | collective-permute-start | bytes 393224 | tf_op jit(solution)/shard_map/ppermute | solution.py:22
  148.9 4.2 %collective-permute-done.24 = bf16[128,512]{1,0:T(8,128)(2,1)S(1)} collective-permute-done((bf16[128,512]{1,0:T(8,128)(2,1)S(1)}, bf16[128,512]{1,0:T(8,128)(2,1)S(1)}, u32[]{:S(2)}, u32[]{:S(2)}) %collective-permute-start.24) | collective-permute-done | bytes 131104 | tf_op jit(solution)/shard_map/ppermute | solution.py:22
  153.3 3.3 %collective-permute-start.29 = (bf16[128,512]{1,0:T(8,128)(2,1)S(1)}, bf16[128,512]{1,0:T(8,128)(2,1)S(1)}, u32[]{:S(2)}, u32[]{:S(2)}) collective-permute-start(bf16[128,512]{1,0:T(8,128)(2,1)S(1)} %add.42), channel_id=1, source_target_pairs={{0,3},{1,0},{2,1},{3,2},{4,7},{5,4},{6,5},{7,6},{8,11},{9,8},{10,9... | collective-permute-start | bytes 393224 | tf_op jit(solution)/shard_map/ppermute | solution.py:22
  156.6 4.1 %collective-permute-done.25 = bf16[128,512]{1,0:T(8,128)(2,1)S(1)} collective-permute-done((bf16[128,512]{1,0:T(8,128)(2,1)S(1)}, bf16[128,512]{1,0:T(8,128)(2,1)S(1)}, u32[]{:S(2)}, u32[]{:S(2)}) %collective-permute-start.25) | collective-permute-done | bytes 131104 | tf_op jit(solution)/shard_map/ppermute | solution.py:22
  (74 shorter events, 22.9 us)
Async XLA Ops:
  1.7 10.5 %collective-permute-start.2 = (bf16[256,512]{1,0:T(8,128)(2,1)S(1)}, bf16[256,512]{1,0:T(8,128)(2,1)S(1)}, u32[]{:S(2)}, u32[]{:S(2)}) collective-permute-start(bf16[256,512]{1,0:T(8,128)(2,1)S(1)} %get-tuple-element.74), channel_id=1, source_target_pairs={{0,1},{1,2},{2,3},{3,0},{4,5},{5,6},{6,7},{7,4},{8,9},{9,10},{10,1... | collective-permute-start | bytes 786440 | tf_op jit(solution)/shard_map/ppermute | solution.py:22
  3.4 9.2 %collective-permute-start.1 = (bf16[256,512]{1,0:T(8,128)(2,1)S(1)}, bf16[256,512]{1,0:T(8,128)(2,1)S(1)}, u32[]{:S(2)}, u32[]{:S(2)}) collective-permute-start(bf16[256,512]{1,0:T(8,128)(2,1)S(1)} %get-tuple-element.73), channel_id=1, source_target_pairs={{0,3},{1,0},{2,1},{3,2},{4,7},{5,4},{6,5},{7,6},{8,11},{9,8},{10,9... | collective-permute-start | bytes 786440 | tf_op jit(solution)/shard_map/ppermute | solution.py:22
  5.0 13.2 %collective-permute-start = (bf16[256,512]{1,0:T(8,128)(2,1)S(1)}, bf16[256,512]{1,0:T(8,128)(2,1)S(1)}, u32[]{:S(2)}, u32[]{:S(2)}) collective-permute-start(bf16[256,512]{1,0:T(8,128)(2,1)S(1)} %get-tuple-element.74), channel_id=1, source_target_pairs={{0,3},{1,0},{2,1},{3,2},{4,7},{5,4},{6,5},{7,6},{8,11},{9,8},{10,9... | collective-permute-start | bytes 786440 | tf_op jit(solution)/shard_map/ppermute | solution.py:22
  6.8 11.4 %collective-permute-start.5 = (bf16[256,512]{1,0:T(8,128)(2,1)S(1)}, bf16[256,512]{1,0:T(8,128)(2,1)S(1)}, u32[]{:S(2)}, u32[]{:S(2)}) collective-permute-start(bf16[256,512]{1,0:T(8,128)(2,1)S(1)} %get-tuple-element.73), channel_id=1, source_target_pairs={{0,1},{1,2},{2,3},{3,0},{4,5},{5,6},{6,7},{7,4},{8,9},{9,10},{10,1... | collective-permute-start | bytes 786440 | tf_op jit(solution)/shard_map/ppermute | solution.py:22
  12.2 10.6 %collective-permute-start.3 = (bf16[256,512]{1,0:T(8,128)(2,1)S(1)}, bf16[256,512]{1,0:T(8,128)(2,1)S(1)}, u32[]{:S(2)}, u32[]{:S(2)}) collective-permute-start(bf16[256,512]{1,0:T(8,128)(2,1)S(1)} %collective-permute-done.2.p3t), channel_id=1, source_target_pairs={{0,1},{1,2},{2,3},{3,0},{4,5},{5,6},{6,7},{7,4},{8,9},{9,10},{10,1... | collective-permute-start | bytes 786440 | tf_op jit(solution)/shard_map/ppermute | solution.py:22
  12.6 10.2 %collective-permute-start.4 = (bf16[256,512]{1,0:T(8,128)(2,1)S(1)}, bf16[256,512]{1,0:T(8,128)(2,1)S(1)}, u32[]{:S(2)}, u32[]{:S(2)}) collective-permute-start(bf16[256,512]{1,0:T(8,128)(2,1)S(1)} %collective-permute-done.1.p1b), channel_id=1, source_target_pairs={{0,3},{1,0},{2,1},{3,2},{4,7},{5,4},{6,5},{7,6},{8,11},{9,8},{10,9... | collective-permute-start | bytes 786440 | tf_op jit(solution)/shard_map/ppermute | solution.py:22
  25.3 13.1 %collective-permute-start.10 = (bf16[320,512]{1,0:T(8,128)(2,1)S(1)}, bf16[320,512]{1,0:T(8,128)(2,1)S(1)}, u32[]{:S(2)}, u32[]{:S(2)}) collective-permute-start(bf16[320,512]{1,0:T(8,128)(2,1)S(1)} %get-tuple-element.45), channel_id=1, source_target_pairs={{0,3},{1,0},{2,1},{3,2},{4,7},{5,4},{6,5},{7,6},{8,11},{9,8},{10,9... | collective-permute-start | bytes 983048 | tf_op jit(solution)/shard_map/ppermute | solution.py:22
  30.2 12.0 %collective-permute-start.6 = (bf16[320,512]{1,0:T(8,128)(2,1)S(1)}, bf16[320,512]{1,0:T(8,128)(2,1)S(1)}, u32[]{:S(2)}, u32[]{:S(2)}) collective-permute-start(bf16[320,512]{1,0:T(8,128)(2,1)S(1)} %get-tuple-element.41), channel_id=1, source_target_pairs={{0,1},{1,2},{2,3},{3,0},{4,5},{5,6},{6,7},{7,4},{8,9},{9,10},{10,1... | collective-permute-start | bytes 983048 | tf_op jit(solution)/shard_map/ppermute | solution.py:22
  30.2 18.6 %collective-permute-start.8 = (bf16[320,512]{1,0:T(8,128)(2,1)S(1)}, bf16[320,512]{1,0:T(8,128)(2,1)S(1)}, u32[]{:S(2)}, u32[]{:S(2)}) collective-permute-start(bf16[320,512]{1,0:T(8,128)(2,1)S(1)} %get-tuple-element.42), channel_id=1, source_target_pairs={{0,1},{1,2},{2,3},{3,0},{4,5},{5,6},{6,7},{7,4},{8,9},{9,10},{10,1... | collective-permute-start | bytes 983048 | tf_op jit(solution)/shard_map/ppermute | solution.py:22
  30.2 18.6 %collective-permute-start.9 = (bf16[320,512]{1,0:T(8,128)(2,1)S(1)}, bf16[320,512]{1,0:T(8,128)(2,1)S(1)}, u32[]{:S(2)}, u32[]{:S(2)}) collective-permute-start(bf16[320,512]{1,0:T(8,128)(2,1)S(1)} %get-tuple-element.43), channel_id=1, source_target_pairs={{0,3},{1,0},{2,1},{3,2},{4,7},{5,4},{6,5},{7,6},{8,11},{9,8},{10,9... | collective-permute-start | bytes 983048 | tf_op jit(solution)/shard_map/ppermute | solution.py:22
  38.4 10.4 %collective-permute-start.11 = (bf16[320,512]{1,0:T(8,128)(2,1)S(1)}, bf16[320,512]{1,0:T(8,128)(2,1)S(1)}, u32[]{:S(2)}, u32[]{:S(2)}) collective-permute-start(bf16[320,512]{1,0:T(8,128)(2,1)S(1)} %add.34), channel_id=1, source_target_pairs={{0,3},{1,0},{2,1},{3,2},{4,7},{5,4},{6,5},{7,6},{8,11},{9,8},{10,9... | collective-permute-start | bytes 983048 | tf_op jit(solution)/shard_map/ppermute | solution.py:22
  42.3 10.0 %collective-permute-start.7 = (bf16[320,512]{1,0:T(8,128)(2,1)S(1)}, bf16[320,512]{1,0:T(8,128)(2,1)S(1)}, u32[]{:S(2)}, u32[]{:S(2)}) collective-permute-start(bf16[320,512]{1,0:T(8,128)(2,1)S(1)} %add.33), channel_id=1, source_target_pairs={{0,1},{1,2},{2,3},{3,0},{4,5},{5,6},{6,7},{7,4},{8,9},{9,10},{10,1... | collective-permute-start | bytes 983048 | tf_op jit(solution)/shard_map/ppermute | solution.py:22
  53.6 14.9 %collective-permute-start.15 = (bf16[512,512]{1,0:T(8,128)(2,1)S(1)}, bf16[512,512]{1,0:T(8,128)(2,1)S(1)}, u32[]{:S(2)}, u32[]{:S(2)}) collective-permute-start(bf16[512,512]{1,0:T(8,128)(2,1)S(1)} %bitcast.23), channel_id=1, source_target_pairs={{0,3},{1,0},{2,1},{3,2},{4,7},{5,4},{6,5},{7,6},{8,11},{9,8},{10,9... | collective-permute-start | bytes 1572872 | tf_op jit(solution)/shard_map/ppermute | solution.py:22
  53.9 16.4 %collective-permute-start.16 = (bf16[512,512]{1,0:T(8,128)(2,1)S(1)}, bf16[512,512]{1,0:T(8,128)(2,1)S(1)}, u32[]{:S(2)}, u32[]{:S(2)}) collective-permute-start(bf16[512,512]{1,0:T(8,128)(2,1)S(1)} %bitcast.24), channel_id=1, source_target_pairs={{0,2},{1,3},{2,0},{3,1},{4,6},{5,7},{6,4},{7,5},{8,10},{9,11},{10,... | collective-permute-start | bytes 1572872 | tf_op jit(solution)/shard_map/ppermute | solution.py:22
  54.7 22.0 %collective-permute-start.17 = (bf16[512,512]{1,0:T(8,128)(2,1)S(1)}, bf16[512,512]{1,0:T(8,128)(2,1)S(1)}, u32[]{:S(2)}, u32[]{:S(2)}) collective-permute-start(bf16[512,512]{1,0:T(8,128)(2,1)S(1)} %bitcast.25), channel_id=1, source_target_pairs={{0,1},{1,2},{2,3},{3,0},{4,5},{5,6},{6,7},{7,4},{8,9},{9,10},{10,1... | collective-permute-start | bytes 1572872 | tf_op jit(solution)/shard_map/ppermute | solution.py:22
  55.6 42.7 %all-to-all-start = ((bf16[64,8,640]{2,1,0:T(8,128)(2,1)}), bf16[64,8,640]{2,1,0:T(8,128)(2,1)S(1)}, u32[]{:S(2)}, u32[]{:S(2)}) async-start(bf16[64,8,640]{2,1,0:T(8,128)(2,1)} %get-tuple-element.48), calls=%async_computation | async-start | bytes 1310720 | tf_op jit(solution)/shard_map/all_to_all | solution.py:421
  81.4 9.0 %collective-permute-start.22 = (bf16[256,512]{1,0:T(8,128)(2,1)S(1)}, bf16[256,512]{1,0:T(8,128)(2,1)S(1)}, u32[]{:S(2)}, u32[]{:S(2)}) collective-permute-start(bf16[256,512]{1,0:T(8,128)(2,1)S(1)} %get-tuple-element.63), channel_id=1, source_target_pairs={{0,3},{1,0},{2,1},{3,2},{4,7},{5,4},{6,5},{7,6},{8,11},{9,8},{10,9... | collective-permute-start | bytes 786440 | tf_op jit(solution)/shard_map/ppermute | solution.py:22
  81.5 11.7 %collective-permute-start.18 = (bf16[256,512]{1,0:T(8,128)(2,1)S(1)}, bf16[256,512]{1,0:T(8,128)(2,1)S(1)}, u32[]{:S(2)}, u32[]{:S(2)}) collective-permute-start(bf16[256,512]{1,0:T(8,128)(2,1)S(1)} %get-tuple-element.59), channel_id=1, source_target_pairs={{0,1},{1,2},{2,3},{3,0},{4,5},{5,6},{6,7},{7,4},{8,9},{9,10},{10,1... | collective-permute-start | bytes 786440 | tf_op jit(solution)/shard_map/ppermute | solution.py:22
  83.5 11.2 %collective-permute-start.12 = (bf16[128,512]{1,0:T(8,128)(2,1)}, bf16[128,512]{1,0:T(8,128)(2,1)S(1)}, u32[]{:S(2)}, u32[]{:S(2)}) collective-permute-start(bf16[128,512]{1,0:T(8,128)(2,1)} %bitcast.9.u0), channel_id=1, source_target_pairs={{0,3},{1,0},{2,1},{3,2},{4,7},{5,4},{6,5},{7,6},{8,11},{9,8},{10,9... | collective-permute-start | bytes 393224 | tf_op jit(solution)/shard_map/ppermute | solution.py:22
  84.8 11.3 %collective-permute-start.13 = (bf16[128,512]{1,0:T(8,128)(2,1)}, bf16[128,512]{1,0:T(8,128)(2,1)S(1)}, u32[]{:S(2)}, u32[]{:S(2)}) collective-permute-start(bf16[128,512]{1,0:T(8,128)(2,1)} %bitcast.9.u0), channel_id=1, source_target_pairs={{0,2},{1,3},{2,0},{3,1},{4,6},{5,7},{6,4},{7,5},{8,10},{9,11},{10,... | collective-permute-start | bytes 393224 | tf_op jit(solution)/shard_map/ppermute | solution.py:22
  86.2 35.0 %collective-permute-start.20 = (bf16[256,512]{1,0:T(8,128)(2,1)S(1)}, bf16[256,512]{1,0:T(8,128)(2,1)S(1)}, u32[]{:S(2)}, u32[]{:S(2)}) collective-permute-start(bf16[256,512]{1,0:T(8,128)(2,1)S(1)} %get-tuple-element.60), channel_id=1, source_target_pairs={{0,1},{1,2},{2,3},{3,0},{4,5},{5,6},{6,7},{7,4},{8,9},{9,10},{10,1... | collective-permute-start | bytes 786440 | tf_op jit(solution)/shard_map/ppermute | solution.py:22
  90.5 30.8 %collective-permute-start.21 = (bf16[256,512]{1,0:T(8,128)(2,1)S(1)}, bf16[256,512]{1,0:T(8,128)(2,1)S(1)}, u32[]{:S(2)}, u32[]{:S(2)}) collective-permute-start(bf16[256,512]{1,0:T(8,128)(2,1)S(1)} %get-tuple-element.61), channel_id=1, source_target_pairs={{0,3},{1,0},{2,1},{3,2},{4,7},{5,4},{6,5},{7,6},{8,11},{9,8},{10,9... | collective-permute-start | bytes 786440 | tf_op jit(solution)/shard_map/ppermute | solution.py:22
  93.2 28.0 %collective-permute-start.23 = (bf16[256,512]{1,0:T(8,128)(2,1)S(1)}, bf16[256,512]{1,0:T(8,128)(2,1)S(1)}, u32[]{:S(2)}, u32[]{:S(2)}) collective-permute-start(bf16[256,512]{1,0:T(8,128)(2,1)S(1)} %add.36), channel_id=1, source_target_pairs={{0,3},{1,0},{2,1},{3,2},{4,7},{5,4},{6,5},{7,6},{8,11},{9,8},{10,9... | collective-permute-start | bytes 786440 | tf_op jit(solution)/shard_map/ppermute | solution.py:22
  94.8 26.5 %collective-permute-start.19 = (bf16[256,512]{1,0:T(8,128)(2,1)}, bf16[256,512]{1,0:T(8,128)(2,1)S(1)}, u32[]{:S(2)}, u32[]{:S(2)}) collective-permute-start(bf16[256,512]{1,0:T(8,128)(2,1)} %add.35), channel_id=1, source_target_pairs={{0,1},{1,2},{2,3},{3,0},{4,5},{5,6},{6,7},{7,4},{8,9},{9,10},{10,1... | collective-permute-start | bytes 786440 | tf_op jit(solution)/shard_map/ppermute | solution.py:22
  96.1 12.7 %collective-permute-start.14 = (bf16[128,512]{1,0:T(8,128)(2,1)}, bf16[128,512]{1,0:T(8,128)(2,1)S(1)}, u32[]{:S(2)}, u32[]{:S(2)}) collective-permute-start(bf16[128,512]{1,0:T(8,128)(2,1)} %bitcast.9.u0), channel_id=1, source_target_pairs={{0,1},{1,2},{2,3},{3,0},{4,5},{5,6},{6,7},{7,4},{8,9},{9,10},{10,1... | collective-permute-start | bytes 393224 | tf_op jit(solution)/shard_map/ppermute | solution.py:22
  108.8 31.7 %all-to-all-start.1 = ((bf16[64,8,640]{2,1,0:T(8,128)(2,1)}), bf16[64,8,640]{2,1,0:T(8,128)(2,1)S(1)}, u32[]{:S(2)}, u32[]{:S(2)}) async-start(bf16[64,8,640]{2,1,0:T(8,128)(2,1)} %pick_parents.1), calls=%async_computation.1 | async-start | bytes 1310720 | tf_op jit(solution)/shard_map/all_to_all | solution.py:427
  145.5 7.5 %collective-permute-start.24 = (bf16[128,512]{1,0:T(8,128)(2,1)S(1)}, bf16[128,512]{1,0:T(8,128)(2,1)S(1)}, u32[]{:S(2)}, u32[]{:S(2)}) collective-permute-start(bf16[128,512]{1,0:T(8,128)(2,1)S(1)} %get-tuple-element.66), channel_id=1, source_target_pairs={{0,1},{1,2},{2,3},{3,0},{4,5},{5,6},{6,7},{7,4},{8,9},{9,10},{10,1... | collective-permute-start | bytes 393224 | tf_op jit(solution)/shard_map/ppermute | solution.py:22
  145.9 7.4 %collective-permute-start.28 = (bf16[128,512]{1,0:T(8,128)(2,1)S(1)}, bf16[128,512]{1,0:T(8,128)(2,1)S(1)}, u32[]{:S(2)}, u32[]{:S(2)}) collective-permute-start(bf16[128,512]{1,0:T(8,128)(2,1)S(1)} %get-tuple-element.72), channel_id=1, source_target_pairs={{0,3},{1,0},{2,1},{3,2},{4,7},{5,4},{6,5},{7,6},{8,11},{9,8},{10,9... | collective-permute-start | bytes 393224 | tf_op jit(solution)/shard_map/ppermute | solution.py:22
  148.8 7.8 %collective-permute-start.26 = (bf16[128,512]{1,0:T(8,128)(2,1)S(1)}, bf16[128,512]{1,0:T(8,128)(2,1)S(1)}, u32[]{:S(2)}, u32[]{:S(2)}) collective-permute-start(bf16[128,512]{1,0:T(8,128)(2,1)S(1)} %get-tuple-element.67), channel_id=1, source_target_pairs={{0,3},{1,0},{2,1},{3,2},{4,7},{5,4},{6,5},{7,6},{8,11},{9,8},{10,9... | collective-permute-start | bytes 393224 | tf_op jit(solution)/shard_map/ppermute | solution.py:22
  153.1 7.7 %collective-permute-start.25 = (bf16[128,512]{1,0:T(8,128)(2,1)S(1)}, bf16[128,512]{1,0:T(8,128)(2,1)S(1)}, u32[]{:S(2)}, u32[]{:S(2)}) collective-permute-start(bf16[128,512]{1,0:T(8,128)(2,1)S(1)} %add.37), channel_id=1, source_target_pairs={{0,1},{1,2},{2,3},{3,0},{4,5},{5,6},{6,7},{7,4},{8,9},{9,10},{10,1... | collective-permute-start | bytes 393224 | tf_op jit(solution)/shard_map/ppermute | solution.py:22
  153.2 9.4 %collective-permute-start.27 = (bf16[128,512]{1,0:T(8,128)(2,1)S(1)}, bf16[128,512]{1,0:T(8,128)(2,1)S(1)}, u32[]{:S(2)}, u32[]{:S(2)}) collective-permute-start(bf16[128,512]{1,0:T(8,128)(2,1)S(1)} %get-tuple-element.70), channel_id=1, source_target_pairs={{0,1},{1,2},{2,3},{3,0},{4,5},{5,6},{6,7},{7,4},{8,9},{9,10},{10,1... | collective-permute-start | bytes 393224 | tf_op jit(solution)/shard_map/ppermute | solution.py:22
  153.3 9.3 %collective-permute-start.29 = (bf16[128,512]{1,0:T(8,128)(2,1)S(1)}, bf16[128,512]{1,0:T(8,128)(2,1)S(1)}, u32[]{:S(2)}, u32[]{:S(2)}) collective-permute-start(bf16[128,512]{1,0:T(8,128)(2,1)S(1)} %add.42), channel_id=1, source_target_pairs={{0,3},{1,0},{2,1},{3,2},{4,7},{5,4},{6,5},{7,6},{8,11},{9,8},{10,9... | collective-permute-start | bytes 393224 | tf_op jit(solution)/shard_map/ppermute | solution.py:22
  (12 other events, 204.6 us)

commit v3 on v2

--- a/solution.py
+++ b/solution.py
@@ -241,7 +241,7 @@
         scratch_shapes=[pltpu.VMEM(square, BF)] + tile_scratch(width, 4),
         compiler_params=pltpu.CompilerParams(vmem_limit_bytes=46 * MIB),
         cost_estimate=pl.CostEstimate(
-            flops=30 * width**3 * 2, bytes_accessed=9 << 20, transcendentals=0
+            flops=40 * width**3 * 2, bytes_accessed=9 << 20, transcendentals=0
         ),
         name="second_products",
     )(ids, ancestors, parents, *lows, root_rows)
@@ -314,19 +314,20 @@
 def sum_kernel(own, left_a, left_b, right_a, right_b, out):
     half = left_a.shape[0]
     for rows, left, right in ((slice(0, half), left_a, right_a), (slice(half, None), left_b, right_b)):
-        out[rows, :] = own[rows, :].astype(F32) + left[...].astype(F32) + right[...].astype(F32)
+        total = own[rows, :].astype(F32) + left[...].astype(F32) + right[...].astype(F32)
+        out[rows, :] = total.astype(BF)
 
 
 def sum_roots(own, received):
     shape = own.shape
     return pl.pallas_call(
         sum_kernel,
-        out_shape=jax.ShapeDtypeStruct(shape, F32),
+        out_shape=jax.ShapeDtypeStruct(shape, BF),
         in_specs=[vmem()] * 5,
         out_specs=vmem(),
         compiler_params=pltpu.CompilerParams(vmem_limit_bytes=VMEM_BYTES),
         cost_estimate=pl.CostEstimate(
-            flops=48 * shape[0] ** 3 * 2, bytes_accessed=3 << 20, transcendentals=0
+            flops=40 * shape[0] ** 3 * 2, bytes_accessed=3 << 20, transcendentals=0
         ),
         name="sum_roots",
     )(own, *received)
@@ -354,7 +355,7 @@
     cross[...] = across
     own = jnp.dot(parent_diag, upper, preferred_element_type=F32)
     lower = jnp.dot(parent_off, upper, preferred_element_type=F32)
-    off_low[...] = -(lower + root[...]).astype(BF)
+    off_low[...] = -(lower + root[...].astype(F32)).astype(BF)
     corr[...] = (
         corr_in[...]
         + rows_dot(u0[...], own.astype(BF))
@@ -416,13 +417,15 @@
     received = scatter_rows(two_a, two_b, next_a, next_b, before_a, before_b)
     off_first, diag_first, slices = settle(mine, received, inverse_first[0], nodes)
     low = panel_lower[0]
-    sent, up = lax.optimization_barrier((low, panel_upper[0], off_first))[:2]
+    sent, up = lax.optimization_barrier((low, panel_upper[0], *received[1:3]))[:2]
     lows, ups = spread_rows(sent), spread_rows(up)
     spread = lax.all_to_all(slices, "snode", split_axis=0, concat_axis=0, tiled=True)
     own, next_a, next_b, two_a, two_b, before_a, before_b, corr = second_products(
         ids, ancestors, parents, lows, root_rows
     )
-    picked, ups = lax.optimization_barrier((pick(parents, spread), ups))
+    picked, next_a, next_b, two_a, two_b, before_a, before_b, ups = lax.optimization_barrier(
+        (pick(parents, spread), next_a, next_b, two_a, two_b, before_a, before_b, ups)
+    )
     received = scatter_rows(two_a, two_b, next_a, next_b, before_a, before_b)
     came = lax.all_to_all(picked, "snode", split_axis=0, concat_axis=0, tiled=True)
     off_low, keep_up, keep_diag, next_a, next_b, two_a, two_b, before_a, before_b = last_products(

time: 164 us -> 150 us (0.915)
  waiting for transfers between devices: 71.1 us -> 54.7 us
  local copies, waits for them, and re-layouts: 7.39 us -> 10.2 us
  starting transfers between devices: 65.2 us -> 62.9 us
  Pallas kernels: 16.2 us -> 18.3 us
    all_to_all x1, waiting for transfers between devices: 17 us -> 2.76 us  [on_device(): lax.all_to_all(picked, 'snode', split_axis=0, concat_axis=0, tiled=True)]
    ppermute x30, waiting for transfers between devices: 54.1 us -> 44.6 us  [shift(): return lax.ppermute(value, 'rows', [(i, (i + step) % n) for i in range(n)])]
    all_to_all x1, waiting for transfers between devices: 0.01 us -> 7.36 us  [on_device(): lax.all_to_all(slices, 'snode', split_axis=0, concat_axis=0, tiled=True)]
    all_to_all x1, starting transfers between devices: 12.4 us -> 7.12 us  [on_device(): lax.all_to_all(picked, 'snode', split_axis=0, concat_axis=0, tiled=True)]
    unnamed x25 -> x29, local copies, waits for them, and re-layouts: 6.32 us -> 9.14 us
    all_to_all x1, starting transfers between devices: 11.2 us -> 13.5 us  [on_device(): lax.all_to_all(slices, 'snode', split_axis=0, concat_axis=0, tiled=True)]
  transfers between devices with their start and end apart: 32 -> 32, of which waited for: 17 -> 13; matrix products, arithmetic and copies ran while one was open for 2% -> 1% of each run, Pallas kernels for 6% -> 8%
where the time goes in v3:
time: 150 us; the launch traced here: 149 us
  starting transfers between devices  62.9 us (42%)
  waiting for transfers between devices  54.7 us (36%)
  Pallas kernels  18.3 us (12%)
  local copies, waits for them, and re-layouts  10.2 us (7%)
  other arithmetic  1.88 us (1%)
    ppermute x30, waiting for transfers between devices, shift(): return lax.ppermute(value, 'rows', [(i, (i + step) % n) for i in range(n)])  44.6 us
    ppermute x30, starting transfers between devices, shift(): return lax.ppermute(value, 'rows', [(i, (i + step) % n) for i in range(n)])  42.2 us
    all_to_all x1, starting transfers between devices, on_device(): lax.all_to_all(slices, 'snode', split_axis=0, concat_axis=0, tiled=True)  13.5 us
    unnamed x29, local copies, waits for them, and re-layouts  9.14 us
    all_to_all x1, waiting for transfers between devices, on_device(): lax.all_to_all(slices, 'snode', split_axis=0, concat_axis=0, tiled=True)  7.36 us
    all_to_all x1, starting transfers between devices, on_device(): lax.all_to_all(picked, 'snode', split_axis=0, concat_axis=0, tiled=True)  7.12 us
    pallas_call x1, Pallas kernels, second_products(): pl.pallas_call(second_kernel, out_shape=[jax.ShapeDtypeStruct(square, BF)...  4.63 us
    pallas_call x1, Pallas kernels, near_products(): pl.pallas_call(near_kernel, out_shape=jax.ShapeDtypeStruct((2 * width, wi...  4.48 us
  transfers between devices with their start and end apart: 32, of which 13 were waited for; matrix products, arithmetic and copies ran while one was open for 1% of the time, Pallas kernels for 8%

profile of v3, /device:TPU:6, one launch (start us, length us, event | category | flops | bytes accessed | tf_op | source)
XLA Modules:
  0.0 148.8 jit_solution(13590560700113073234)
XLA Ops:
  1.7 1.7 %collective-permute-start.2 = (bf16[256,512]{1,0:T(8,128)(2,1)S(1)}, bf16[256,512]{1,0:T(8,128)(2,1)S(1)}, u32[]{:S(2)}, u32[]{:S(2)}) collective-permute-start(bf16[256,512]{1,0:T(8,128)(2,1)S(1)} %get-tuple-element.86), channel_id=1, source_target_pairs={{0,1},{1,2},{2,3},{3,0},{4,5},{5,6},{6,7},{7,4},{8,9},{9,10},{10,1... | collective-permute-start | bytes 786440 | tf_op jit(solution)/shard_map/ppermute | solution.py:22
  3.4 1.7 %collective-permute-start.1 = (bf16[256,512]{1,0:T(8,128)(2,1)S(1)}, bf16[256,512]{1,0:T(8,128)(2,1)S(1)}, u32[]{:S(2)}, u32[]{:S(2)}) collective-permute-start(bf16[256,512]{1,0:T(8,128)(2,1)S(1)} %get-tuple-element.85), channel_id=1, source_target_pairs={{0,3},{1,0},{2,1},{3,2},{4,7},{5,4},{6,5},{7,6},{8,11},{9,8},{10,9... | collective-permute-start | bytes 786440 | tf_op jit(solution)/shard_map/ppermute | solution.py:22
  5.0 1.8 %collective-permute-start = (bf16[256,512]{1,0:T(8,128)(2,1)S(1)}, bf16[256,512]{1,0:T(8,128)(2,1)S(1)}, u32[]{:S(2)}, u32[]{:S(2)}) collective-permute-start(bf16[256,512]{1,0:T(8,128)(2,1)S(1)} %get-tuple-element.86), channel_id=1, source_target_pairs={{0,3},{1,0},{2,1},{3,2},{4,7},{5,4},{6,5},{7,6},{8,11},{9,8},{10,9... | collective-permute-start | bytes 786440 | tf_op jit(solution)/shard_map/ppermute | solution.py:22
  7.8 4.4 %collective-permute-done.2.p3t = bf16[256,512]{1,0:T(8,128)(2,1)S(1)} collective-permute-done((bf16[256,512]{1,0:T(8,128)(2,1)S(1)}, bf16[256,512]{1,0:T(8,128)(2,1)S(1)}, u32[]{:S(2)}, u32[]{:S(2)}) %collective-permute-start.2) | collective-permute-done | bytes 262176 | tf_op jit(solution)/shard_map/ppermute | solution.py:22
  12.6 2.8 %collective-permute-start.4 = (bf16[256,512]{1,0:T(8,128)(2,1)S(1)}, bf16[256,512]{1,0:T(8,128)(2,1)S(1)}, u32[]{:S(2)}, u32[]{:S(2)}) collective-permute-start(bf16[256,512]{1,0:T(8,128)(2,1)S(1)} %collective-permute-done.1.p1b), channel_id=1, source_target_pairs={{0,3},{1,0},{2,1},{3,2},{4,7},{5,4},{6,5},{7,6},{8,11},{9,8},{10,9... | collective-permute-start | bytes 786440 | tf_op jit(solution)/shard_map/ppermute | solution.py:22
  15.5 2.7 %collective-permute-done.p1t = bf16[256,512]{1,0:T(8,128)(2,1)S(1)} collective-permute-done((bf16[256,512]{1,0:T(8,128)(2,1)S(1)}, bf16[256,512]{1,0:T(8,128)(2,1)S(1)}, u32[]{:S(2)}, u32[]{:S(2)}) %collective-permute-start) | collective-permute-done | bytes 262176 | tf_op jit(solution)/shard_map/ppermute | solution.py:22
  19.3 4.5 %near_products.1.near = f32[1024,512]{1,0:T(8,128)S(1)} custom-call(s32[2]{0:T(128)S(1)} %pad_add_fusion.ids, s32[64,4]{1,0:T(8,128)S(1)} %copy.14.anc, bf16[512,512]{1,0:T(8,128)(2,1)S(1)} %bitcast.20, bf16[256,512]{1,0:T(8,128)(2,1)S(1)} %collective-permute-done.p1t, bf16[256,512]{1,0:T(8,128)(2,1)S(1)} %collective-permute-done.1.p1b, ...), custom_call_target="tpu_custom_call" | custom-call | flops 1610612736 | bytes 6291456 | tf_op jit(solution)/shard_map/near_products/pallas_call | solution.py:161
  23.8 3.5 %first_products.1 = (bf16[640,512]{1,0:T(8,128)(2,1)S(1)}, bf16[320,512]{1,0:T(8,128)(2,1)S(1)}, bf16[320,512]{1,0:T(8,128)(2,1)S(1)}, bf16[320,512]{1,0:T(8,128...) custom-call(s32[2]{0:T(128)S(1)} %pad_add_fusion.ids, ...), custom_call_target="tpu_custom_call" | custom-call | flops 1073741824 | bytes 8388608 | tf_op jit(solution)/shard_map/first_products/pallas_call | solution.py:180
  27.4 3.2 %collective-permute-start.10 = (bf16[320,512]{1,0:T(8,128)(2,1)S(1)}, bf16[320,512]{1,0:T(8,128)(2,1)S(1)}, u32[]{:S(2)}, u32[]{:S(2)}) collective-permute-start(bf16[320,512]{1,0:T(8,128)(2,1)S(1)} %get-tuple-element.51), channel_id=1, source_target_pairs={{0,3},{1,0},{2,1},{3,2},{4,7},{5,4},{6,5},{7,6},{8,11},{9,8},{10,9... | collective-permute-start | bytes 983048 | tf_op jit(solution)/shard_map/ppermute | solution.py:22
  30.6 3.2 %collective-permute-start.9 = (bf16[320,512]{1,0:T(8,128)(2,1)S(1)}, bf16[320,512]{1,0:T(8,128)(2,1)S(1)}, u32[]{:S(2)}, u32[]{:S(2)}) collective-permute-start(bf16[320,512]{1,0:T(8,128)(2,1)S(1)} %get-tuple-element.49), channel_id=1, source_target_pairs={{0,3},{1,0},{2,1},{3,2},{4,7},{5,4},{6,5},{7,6},{8,11},{9,8},{10,9... | collective-permute-start | bytes 983048 | tf_op jit(solution)/shard_map/ppermute | solution.py:22
  33.8 5.4 %collective-permute-done.6 = bf16[320,512]{1,0:T(8,128)(2,1)S(1)} collective-permute-done((bf16[320,512]{1,0:T(8,128)(2,1)S(1)}, bf16[320,512]{1,0:T(8,128)(2,1)S(1)}, u32[]{:S(2)}, u32[]{:S(2)}) %collective-permute-start.6) | collective-permute-done | bytes 327712 | tf_op jit(solution)/shard_map/ppermute | solution.py:22
  39.5 3.3 %collective-permute-start.11 = (bf16[320,512]{1,0:T(8,128)(2,1)S(1)}, bf16[320,512]{1,0:T(8,128)(2,1)S(1)}, u32[]{:S(2)}, u32[]{:S(2)}) collective-permute-start(bf16[320,512]{1,0:T(8,128)(2,1)S(1)} %add.34), channel_id=1, source_target_pairs={{0,3},{1,0},{2,1},{3,2},{4,7},{5,4},{6,5},{7,6},{8,11},{9,8},{10,9... | collective-permute-start | bytes 983048 | tf_op jit(solution)/shard_map/ppermute | solution.py:22
  42.8 2.6 %collective-permute-done.8.left_b = bf16[320,512]{1,0:T(8,128)(2,1)S(1)} collective-permute-done((bf16[320,512]{1,0:T(8,128)(2,1)S(1)}, bf16[320,512]{1,0:T(8,128)(2,1)S(1)}, u32[]{:S(2)}, u32[]{:S(2)}) %collective-permute-start.8) | collective-permute-done | bytes 327712 | tf_op jit(solution)/shard_map/ppermute | solution.py:22
  45.8 3.7 %collective-permute-start.12 = (bf16[512,512]{1,0:T(8,128)(2,1)S(1)}, bf16[512,512]{1,0:T(8,128)(2,1)S(1)}, u32[]{:S(2)}, u32[]{:S(2)}) collective-permute-start(bf16[512,512]{1,0:T(8,128)(2,1)S(1)} %bitcast.23), channel_id=1, source_target_pairs={{0,3},{1,0},{2,1},{3,2},{4,7},{5,4},{6,5},{7,6},{8,11},{9,8},{10,9... | collective-permute-start | bytes 1572872 | tf_op jit(solution)/shard_map/ppermute | solution.py:22
  50.3 11.2 %collective-permute-done.7.left_a = bf16[320,512]{1,0:T(8,128)(2,1)S(1)} collective-permute-done((bf16[320,512]{1,0:T(8,128)(2,1)S(1)}, bf16[320,512]{1,0:T(8,128)(2,1)S(1)}, u32[]{:S(2)}, u32[]{:S(2)}) %collective-permute-start.7) | collective-permute-done | bytes 327712 | tf_op jit(solution)/shard_map/ppermute | solution.py:22
  62.8 13.5 %all-to-all-start = ((bf16[64,8,640]{2,1,0:T(8,128)(2,1)}), bf16[64,8,640]{2,1,0:T(8,128)(2,1)S(1)}, u32[]{:S(2)}, u32[]{:S(2)}) async-start(bf16[64,8,640]{2,1,0:T(8,128)(2,1)} %get-tuple-element.54), calls=%async_computation | async-start | bytes 1310720 | tf_op jit(solution)/shard_map/all_to_all | solution.py:422
  77.2 1.3 collective-permute-start.17
  80.4 4.6 %second_products.1 = (bf16[512,512]{1,0:T(8,128)(2,1)S(1)}, bf16[256,512]{1,0:T(8,128)(2,1)S(1)}, bf16[256,512]{1,0:T(8,128)(2,1)S(1)}, bf16[256,512]{1,0:T(8,12...) custom-call(s32[2]{0:T(128)S(1)} %pad_add_fusion.ids, ...), custom_call_target="tpu_custom_call" | custom-call | flops 10737418240 | bytes 9437184 | tf_op jit(solution)/shard_map/second_products/pallas_call | solution.py:234
  88.2 7.4 %all-to-all-done.held = bf16[64,8,640]{2,1,0:T(8,128)(2,1)S(1)} async-done(((bf16[64,8,640]{2,1,0:T(8,128)(2,1)}), bf16[64,8,640]{2,1,0:T(8,128)(2,1)S(1)}, u32[]{:S(2)}, u32[]{:S(2)}) %all-to-all-start) | async-done | bytes 655392 | tf_op jit(solution)/shard_map/all_to_all | solution.py:422
  95.6 1.5 pick_parents.1
  97.4 3.2 %collective-permute-start.22 = (bf16[256,512]{1,0:T(8,128)(2,1)}, bf16[256,512]{1,0:T(8,128)(2,1)S(1)}, u32[]{:S(2)}, u32[]{:S(2)}) collective-permute-start(bf16[256,512]{1,0:T(8,128)(2,1)} %copy-done.7), channel_id=1, source_target_pairs={{0,3},{1,0},{2,1},{3,2},{4,7},{5,4},{6,5},{7,6},{8,11},{9,8},{10,9... | collective-permute-start | bytes 786440 | tf_op jit(solution)/shard_map/ppermute | solution.py:22
  100.6 7.1 %all-to-all-start.1 = ((bf16[64,8,640]{2,1,0:T(8,128)(2,1)}), bf16[64,8,640]{2,1,0:T(8,128)(2,1)S(1)}, u32[]{:S(2)}, u32[]{:S(2)}) async-start(bf16[64,8,640]{2,1,0:T(8,128)(2,1)} %pick_parents.1), calls=%async_computation.1 | async-start | bytes 1310720 | tf_op jit(solution)/shard_map/all_to_all | solution.py:430
  107.8 3.2 %collective-permute-start.21 = (bf16[256,512]{1,0:T(8,128)(2,1)S(1)}, bf16[256,512]{1,0:T(8,128)(2,1)S(1)}, u32[]{:S(2)}, u32[]{:S(2)}) collective-permute-start(bf16[256,512]{1,0:T(8,128)(2,1)S(1)} %get-tuple-element.73), channel_id=1, source_target_pairs={{0,3},{1,0},{2,1},{3,2},{4,7},{5,4},{6,5},{7,6},{8,11},{9,8},{10,9... | collective-permute-start | bytes 786440 | tf_op jit(solution)/shard_map/ppermute | solution.py:22
  111.3 3.3 %collective-permute-start.23 = (bf16[256,512]{1,0:T(8,128)(2,1)S(1)}, bf16[256,512]{1,0:T(8,128)(2,1)S(1)}, u32[]{:S(2)}, u32[]{:S(2)}) collective-permute-start(bf16[256,512]{1,0:T(8,128)(2,1)S(1)} %add.36), channel_id=1, source_target_pairs={{0,3},{1,0},{2,1},{3,2},{4,7},{5,4},{6,5},{7,6},{8,11},{9,8},{10,9... | collective-permute-start | bytes 786440 | tf_op jit(solution)/shard_map/ppermute | solution.py:22
  114.6 3.6 %collective-permute-done.20.left_b = bf16[256,512]{1,0:T(8,128)(2,1)S(1)} collective-permute-done((bf16[256,512]{1,0:T(8,128)(2,1)S(1)}, bf16[256,512]{1,0:T(8,128)(2,1)S(1)}, u32[]{:S(2)}, u32[]{:S(2)}) %collective-permute-start.20) | collective-permute-done | bytes 262176 | tf_op jit(solution)/shard_map/ppermute | solution.py:22
  118.2 4.8 %collective-permute-done.19.left_a = bf16[256,512]{1,0:T(8,128)(2,1)S(1)} collective-permute-done((bf16[256,512]{1,0:T(8,128)(2,1)S(1)}, bf16[256,512]{1,0:T(8,128)(2,1)S(1)}, u32[]{:S(2)}, u32[]{:S(2)}) %collective-permute-start.19) | collective-permute-done | bytes 262176 | tf_op jit(solution)/shard_map/ppermute | solution.py:22
  124.2 2.8 %all-to-all-done.1.came = bf16[64,8,640]{2,1,0:T(8,128)(2,1)S(1)} async-done(((bf16[64,8,640]{2,1,0:T(8,128)(2,1)}), bf16[64,8,640]{2,1,0:T(8,128)(2,1)S(1)}, u32[]{:S(2)}, u32[]{:S(2)}) %all-to-all-start.1) | async-done | bytes 655392 | tf_op jit(solution)/shard_map/all_to_all | solution.py:430
  128.2 2.8 %last_products.1 = (bf16[512,512]{1,0:T(8,128)(2,1)}, f32[128,512]{1,0:T(8,128)S(1)}, f32[128,512]{1,0:T(8,128)S(1)}, bf16[128,512]{1,0:T(8,128)(2,1)S(1)}, bf16...) custom-call(s32[2]{0:T(128)S(1)} %pad_add_fusion.ids, ...), custom_call_target="tpu_custom_call" | custom-call | flops 1342177280 | bytes 6291456 | tf_op jit(solution)/shard_map/last_products/pallas_call | solution.py:382
  131.1 3.2 %collective-permute-start.28 = (bf16[128,512]{1,0:T(8,128)(2,1)S(1)}, bf16[128,512]{1,0:T(8,128)(2,1)S(1)}, u32[]{:S(2)}, u32[]{:S(2)}) collective-permute-start(bf16[128,512]{1,0:T(8,128)(2,1)S(1)} %get-tuple-element.84), channel_id=1, source_target_pairs={{0,3},{1,0},{2,1},{3,2},{4,7},{5,4},{6,5},{7,6},{8,11},{9,8},{10,9... | collective-permute-start | bytes 393224 | tf_op jit(solution)/shard_map/ppermute | solution.py:22
  134.4 4.2 %collective-permute-done.24 = bf16[128,512]{1,0:T(8,128)(2,1)S(1)} collective-permute-done((bf16[128,512]{1,0:T(8,128)(2,1)S(1)}, bf16[128,512]{1,0:T(8,128)(2,1)S(1)}, u32[]{:S(2)}, u32[]{:S(2)}) %collective-permute-start.24) | collective-permute-done | bytes 131104 | tf_op jit(solution)/shard_map/ppermute | solution.py:22
  138.8 3.3 %collective-permute-start.29 = (bf16[128,512]{1,0:T(8,128)(2,1)S(1)}, bf16[128,512]{1,0:T(8,128)(2,1)S(1)}, u32[]{:S(2)}, u32[]{:S(2)}) collective-permute-start(bf16[128,512]{1,0:T(8,128)(2,1)S(1)} %add.42), channel_id=1, source_target_pairs={{0,3},{1,0},{2,1},{3,2},{4,7},{5,4},{6,5},{7,6},{8,11},{9,8},{10,9... | collective-permute-start | bytes 393224 | tf_op jit(solution)/shard_map/ppermute | solution.py:22
  142.1 4.1 %collective-permute-done.25 = bf16[128,512]{1,0:T(8,128)(2,1)S(1)} collective-permute-done((bf16[128,512]{1,0:T(8,128)(2,1)S(1)}, bf16[128,512]{1,0:T(8,128)(2,1)S(1)}, u32[]{:S(2)}, u32[]{:S(2)}) %collective-permute-start.25) | collective-permute-done | bytes 131104 | tf_op jit(solution)/shard_map/ppermute | solution.py:22
  (78 shorter events, 18.3 us)
Async XLA Ops:
  1.7 10.5 %collective-permute-start.2 = (bf16[256,512]{1,0:T(8,128)(2,1)S(1)}, bf16[256,512]{1,0:T(8,128)(2,1)S(1)}, u32[]{:S(2)}, u32[]{:S(2)}) collective-permute-start(bf16[256,512]{1,0:T(8,128)(2,1)S(1)} %get-tuple-element.86), channel_id=1, source_target_pairs={{0,1},{1,2},{2,3},{3,0},{4,5},{5,6},{6,7},{7,4},{8,9},{9,10},{10,1... | collective-permute-start | bytes 786440 | tf_op jit(solution)/shard_map/ppermute | solution.py:22
  3.4 9.2 %collective-permute-start.1 = (bf16[256,512]{1,0:T(8,128)(2,1)S(1)}, bf16[256,512]{1,0:T(8,128)(2,1)S(1)}, u32[]{:S(2)}, u32[]{:S(2)}) collective-permute-start(bf16[256,512]{1,0:T(8,128)(2,1)S(1)} %get-tuple-element.85), channel_id=1, source_target_pairs={{0,3},{1,0},{2,1},{3,2},{4,7},{5,4},{6,5},{7,6},{8,11},{9,8},{10,9... | collective-permute-start | bytes 786440 | tf_op jit(solution)/shard_map/ppermute | solution.py:22
  5.0 13.2 %collective-permute-start = (bf16[256,512]{1,0:T(8,128)(2,1)S(1)}, bf16[256,512]{1,0:T(8,128)(2,1)S(1)}, u32[]{:S(2)}, u32[]{:S(2)}) collective-permute-start(bf16[256,512]{1,0:T(8,128)(2,1)S(1)} %get-tuple-element.86), channel_id=1, source_target_pairs={{0,3},{1,0},{2,1},{3,2},{4,7},{5,4},{6,5},{7,6},{8,11},{9,8},{10,9... | collective-permute-start | bytes 786440 | tf_op jit(solution)/shard_map/ppermute | solution.py:22
  6.8 11.4 %collective-permute-start.5 = (bf16[256,512]{1,0:T(8,128)(2,1)S(1)}, bf16[256,512]{1,0:T(8,128)(2,1)S(1)}, u32[]{:S(2)}, u32[]{:S(2)}) collective-permute-start(bf16[256,512]{1,0:T(8,128)(2,1)S(1)} %get-tuple-element.85), channel_id=1, source_target_pairs={{0,1},{1,2},{2,3},{3,0},{4,5},{5,6},{6,7},{7,4},{8,9},{9,10},{10,1... | collective-permute-start | bytes 786440 | tf_op jit(solution)/shard_map/ppermute | solution.py:22
  12.2 11.6 %collective-permute-start.3 = (bf16[256,512]{1,0:T(8,128)(2,1)S(1)}, bf16[256,512]{1,0:T(8,128)(2,1)S(1)}, u32[]{:S(2)}, u32[]{:S(2)}) collective-permute-start(bf16[256,512]{1,0:T(8,128)(2,1)S(1)} %collective-permute-done.2.p3t), channel_id=1, source_target_pairs={{0,1},{1,2},{2,3},{3,0},{4,5},{5,6},{6,7},{7,4},{8,9},{9,10},{10,1... | collective-permute-start | bytes 786440 | tf_op jit(solution)/shard_map/ppermute | solution.py:22
  12.6 11.2 %collective-permute-start.4 = (bf16[256,512]{1,0:T(8,128)(2,1)S(1)}, bf16[256,512]{1,0:T(8,128)(2,1)S(1)}, u32[]{:S(2)}, u32[]{:S(2)}) collective-permute-start(bf16[256,512]{1,0:T(8,128)(2,1)S(1)} %collective-permute-done.1.p1b), channel_id=1, source_target_pairs={{0,3},{1,0},{2,1},{3,2},{4,7},{5,4},{6,5},{7,6},{8,11},{9,8},{10,9... | collective-permute-start | bytes 786440 | tf_op jit(solution)/shard_map/ppermute | solution.py:22
  27.3 11.9 %collective-permute-start.6 = (bf16[320,512]{1,0:T(8,128)(2,1)S(1)}, bf16[320,512]{1,0:T(8,128)(2,1)S(1)}, u32[]{:S(2)}, u32[]{:S(2)}) collective-permute-start(bf16[320,512]{1,0:T(8,128)(2,1)S(1)} %get-tuple-element.47), channel_id=1, source_target_pairs={{0,1},{1,2},{2,3},{3,0},{4,5},{5,6},{6,7},{7,4},{8,9},{9,10},{10,1... | collective-permute-start | bytes 983048 | tf_op jit(solution)/shard_map/ppermute | solution.py:22
  27.4 12.0 %collective-permute-start.10 = (bf16[320,512]{1,0:T(8,128)(2,1)S(1)}, bf16[320,512]{1,0:T(8,128)(2,1)S(1)}, u32[]{:S(2)}, u32[]{:S(2)}) collective-permute-start(bf16[320,512]{1,0:T(8,128)(2,1)S(1)} %get-tuple-element.51), channel_id=1, source_target_pairs={{0,3},{1,0},{2,1},{3,2},{4,7},{5,4},{6,5},{7,6},{8,11},{9,8},{10,9... | collective-permute-start | bytes 983048 | tf_op jit(solution)/shard_map/ppermute | solution.py:22
  30.6 14.8 %collective-permute-start.8 = (bf16[320,512]{1,0:T(8,128)(2,1)S(1)}, bf16[320,512]{1,0:T(8,128)(2,1)S(1)}, u32[]{:S(2)}, u32[]{:S(2)}) collective-permute-start(bf16[320,512]{1,0:T(8,128)(2,1)S(1)} %get-tuple-element.48), channel_id=1, source_target_pairs={{0,1},{1,2},{2,3},{3,0},{4,5},{5,6},{6,7},{7,4},{8,9},{9,10},{10,1... | collective-permute-start | bytes 983048 | tf_op jit(solution)/shard_map/ppermute | solution.py:22
  30.6 15.2 %collective-permute-start.9 = (bf16[320,512]{1,0:T(8,128)(2,1)S(1)}, bf16[320,512]{1,0:T(8,128)(2,1)S(1)}, u32[]{:S(2)}, u32[]{:S(2)}) collective-permute-start(bf16[320,512]{1,0:T(8,128)(2,1)S(1)} %get-tuple-element.49), channel_id=1, source_target_pairs={{0,3},{1,0},{2,1},{3,2},{4,7},{5,4},{6,5},{7,6},{8,11},{9,8},{10,9... | collective-permute-start | bytes 983048 | tf_op jit(solution)/shard_map/ppermute | solution.py:22
  39.3 22.2 %collective-permute-start.7 = (bf16[320,512]{1,0:T(8,128)(2,1)S(1)}, bf16[320,512]{1,0:T(8,128)(2,1)S(1)}, u32[]{:S(2)}, u32[]{:S(2)}) collective-permute-start(bf16[320,512]{1,0:T(8,128)(2,1)S(1)} %add.33), channel_id=1, source_target_pairs={{0,1},{1,2},{2,3},{3,0},{4,5},{5,6},{6,7},{7,4},{8,9},{9,10},{10,1... | collective-permute-start | bytes 983048 | tf_op jit(solution)/shard_map/ppermute | solution.py:22
  39.5 22.0 %collective-permute-start.11 = (bf16[320,512]{1,0:T(8,128)(2,1)S(1)}, bf16[320,512]{1,0:T(8,128)(2,1)S(1)}, u32[]{:S(2)}, u32[]{:S(2)}) collective-permute-start(bf16[320,512]{1,0:T(8,128)(2,1)S(1)} %add.34), channel_id=1, source_target_pairs={{0,3},{1,0},{2,1},{3,2},{4,7},{5,4},{6,5},{7,6},{8,11},{9,8},{10,9... | collective-permute-start | bytes 983048 | tf_op jit(solution)/shard_map/ppermute | solution.py:22
  45.8 31.4 %collective-permute-start.12 = (bf16[512,512]{1,0:T(8,128)(2,1)S(1)}, bf16[512,512]{1,0:T(8,128)(2,1)S(1)}, u32[]{:S(2)}, u32[]{:S(2)}) collective-permute-start(bf16[512,512]{1,0:T(8,128)(2,1)S(1)} %bitcast.23), channel_id=1, source_target_pairs={{0,3},{1,0},{2,1},{3,2},{4,7},{5,4},{6,5},{7,6},{8,11},{9,8},{10,9... | collective-permute-start | bytes 1572872 | tf_op jit(solution)/shard_map/ppermute | solution.py:22
  49.5 29.0 %collective-permute-start.13 = (bf16[512,512]{1,0:T(8,128)(2,1)S(1)}, bf16[512,512]{1,0:T(8,128)(2,1)S(1)}, u32[]{:S(2)}, u32[]{:S(2)}) collective-permute-start(bf16[512,512]{1,0:T(8,128)(2,1)S(1)} %bitcast.24), channel_id=1, source_target_pairs={{0,2},{1,3},{2,0},{3,1},{4,6},{5,7},{6,4},{7,5},{8,10},{9,11},{10,... | collective-permute-start | bytes 1572872 | tf_op jit(solution)/shard_map/ppermute | solution.py:22
  49.5 29.0 %collective-permute-start.14 = (bf16[512,512]{1,0:T(8,128)(2,1)S(1)}, bf16[512,512]{1,0:T(8,128)(2,1)S(1)}, u32[]{:S(2)}, u32[]{:S(2)}) collective-permute-start(bf16[512,512]{1,0:T(8,128)(2,1)S(1)} %bitcast.25), channel_id=1, source_target_pairs={{0,1},{1,2},{2,3},{3,0},{4,5},{5,6},{6,7},{7,4},{8,9},{9,10},{10,1... | collective-permute-start | bytes 1572872 | tf_op jit(solution)/shard_map/ppermute | solution.py:22
  62.8 32.8 %all-to-all-start = ((bf16[64,8,640]{2,1,0:T(8,128)(2,1)}), bf16[64,8,640]{2,1,0:T(8,128)(2,1)S(1)}, u32[]{:S(2)}, u32[]{:S(2)}) async-start(bf16[64,8,640]{2,1,0:T(8,128)(2,1)} %get-tuple-element.54), calls=%async_computation | async-start | bytes 1310720 | tf_op jit(solution)/shard_map/all_to_all | solution.py:422
  76.3 20.8 %collective-permute-start.15 = (bf16[128,512]{1,0:T(8,128)(2,1)}, bf16[128,512]{1,0:T(8,128)(2,1)}, u32[]{:S(2)}, u32[]{:S(2)}) collective-permute-start(bf16[128,512]{1,0:T(8,128)(2,1)} %bitcast.9.u0), channel_id=1, source_target_pairs={{0,3},{1,0},{2,1},{3,2},{4,7},{5,4},{6,5},{7,6},{8,11},{9,8},{10,9... | collective-permute-start | bytes 393224 | tf_op jit(solution)/shard_map/ppermute | solution.py:22
  76.4 20.7 %collective-permute-start.16 = (bf16[128,512]{1,0:T(8,128)(2,1)}, bf16[128,512]{1,0:T(8,128)(2,1)}, u32[]{:S(2)}, u32[]{:S(2)}) collective-permute-start(bf16[128,512]{1,0:T(8,128)(2,1)} %bitcast.9.u0), channel_id=1, source_target_pairs={{0,2},{1,3},{2,0},{3,1},{4,6},{5,7},{6,4},{7,5},{8,10},{9,11},{10,... | collective-permute-start | bytes 393224 | tf_op jit(solution)/shard_map/ppermute | solution.py:22
  77.2 19.9 %collective-permute-start.17 = (bf16[128,512]{1,0:T(8,128)(2,1)}, bf16[128,512]{1,0:T(8,128)(2,1)}, u32[]{:S(2)}, u32[]{:S(2)}) collective-permute-start(bf16[128,512]{1,0:T(8,128)(2,1)} %bitcast.9.u0), channel_id=1, source_target_pairs={{0,1},{1,2},{2,3},{3,0},{4,5},{5,6},{6,7},{7,4},{8,9},{9,10},{10,1... | collective-permute-start | bytes 393224 | tf_op jit(solution)/shard_map/ppermute | solution.py:22
  97.1 14.0 %collective-permute-start.18 = (bf16[256,512]{1,0:T(8,128)(2,1)}, bf16[256,512]{1,0:T(8,128)(2,1)S(1)}, u32[]{:S(2)}, u32[]{:S(2)}) collective-permute-start(bf16[256,512]{1,0:T(8,128)(2,1)} %copy-done.8), channel_id=1, source_target_pairs={{0,1},{1,2},{2,3},{3,0},{4,5},{5,6},{6,7},{7,4},{8,9},{9,10},{10,1... | collective-permute-start | bytes 786440 | tf_op jit(solution)/shard_map/ppermute | solution.py:22
  97.4 13.8 %collective-permute-start.22 = (bf16[256,512]{1,0:T(8,128)(2,1)}, bf16[256,512]{1,0:T(8,128)(2,1)S(1)}, u32[]{:S(2)}, u32[]{:S(2)}) collective-permute-start(bf16[256,512]{1,0:T(8,128)(2,1)} %copy-done.7), channel_id=1, source_target_pairs={{0,3},{1,0},{2,1},{3,2},{4,7},{5,4},{6,5},{7,6},{8,11},{9,8},{10,9... | collective-permute-start | bytes 786440 | tf_op jit(solution)/shard_map/ppermute | solution.py:22
  100.6 26.4 %all-to-all-start.1 = ((bf16[64,8,640]{2,1,0:T(8,128)(2,1)}), bf16[64,8,640]{2,1,0:T(8,128)(2,1)S(1)}, u32[]{:S(2)}, u32[]{:S(2)}) async-start(bf16[64,8,640]{2,1,0:T(8,128)(2,1)} %pick_parents.1), calls=%async_computation.1 | async-start | bytes 1310720 | tf_op jit(solution)/shard_map/all_to_all | solution.py:430
  107.7 10.4 %collective-permute-start.20 = (bf16[256,512]{1,0:T(8,128)(2,1)S(1)}, bf16[256,512]{1,0:T(8,128)(2,1)S(1)}, u32[]{:S(2)}, u32[]{:S(2)}) collective-permute-start(bf16[256,512]{1,0:T(8,128)(2,1)S(1)} %get-tuple-element.72), channel_id=1, source_target_pairs={{0,1},{1,2},{2,3},{3,0},{4,5},{5,6},{6,7},{7,4},{8,9},{9,10},{10,1... | collective-permute-start | bytes 786440 | tf_op jit(solution)/shard_map/ppermute | solution.py:22
  107.8 10.3 %collective-permute-start.21 = (bf16[256,512]{1,0:T(8,128)(2,1)S(1)}, bf16[256,512]{1,0:T(8,128)(2,1)S(1)}, u32[]{:S(2)}, u32[]{:S(2)}) collective-permute-start(bf16[256,512]{1,0:T(8,128)(2,1)S(1)} %get-tuple-element.73), channel_id=1, source_target_pairs={{0,3},{1,0},{2,1},{3,2},{4,7},{5,4},{6,5},{7,6},{8,11},{9,8},{10,9... | collective-permute-start | bytes 786440 | tf_op jit(solution)/shard_map/ppermute | solution.py:22
  111.1 11.9 %collective-permute-start.19 = (bf16[256,512]{1,0:T(8,128)(2,1)S(1)}, bf16[256,512]{1,0:T(8,128)(2,1)S(1)}, u32[]{:S(2)}, u32[]{:S(2)}) collective-permute-start(bf16[256,512]{1,0:T(8,128)(2,1)S(1)} %add.35), channel_id=1, source_target_pairs={{0,1},{1,2},{2,3},{3,0},{4,5},{5,6},{6,7},{7,4},{8,9},{9,10},{10,1... | collective-permute-start | bytes 786440 | tf_op jit(solution)/shard_map/ppermute | solution.py:22
  111.3 11.7 %collective-permute-start.23 = (bf16[256,512]{1,0:T(8,128)(2,1)S(1)}, bf16[256,512]{1,0:T(8,128)(2,1)S(1)}, u32[]{:S(2)}, u32[]{:S(2)}) collective-permute-start(bf16[256,512]{1,0:T(8,128)(2,1)S(1)} %add.36), channel_id=1, source_target_pairs={{0,3},{1,0},{2,1},{3,2},{4,7},{5,4},{6,5},{7,6},{8,11},{9,8},{10,9... | collective-permute-start | bytes 786440 | tf_op jit(solution)/shard_map/ppermute | solution.py:22
  131.0 7.5 %collective-permute-start.24 = (bf16[128,512]{1,0:T(8,128)(2,1)S(1)}, bf16[128,512]{1,0:T(8,128)(2,1)S(1)}, u32[]{:S(2)}, u32[]{:S(2)}) collective-permute-start(bf16[128,512]{1,0:T(8,128)(2,1)S(1)} %get-tuple-element.78), channel_id=1, source_target_pairs={{0,1},{1,2},{2,3},{3,0},{4,5},{5,6},{6,7},{7,4},{8,9},{9,10},{10,1... | collective-permute-start | bytes 393224 | tf_op jit(solution)/shard_map/ppermute | solution.py:22
  131.1 7.7 %collective-permute-start.28 = (bf16[128,512]{1,0:T(8,128)(2,1)S(1)}, bf16[128,512]{1,0:T(8,128)(2,1)S(1)}, u32[]{:S(2)}, u32[]{:S(2)}) collective-permute-start(bf16[128,512]{1,0:T(8,128)(2,1)S(1)} %get-tuple-element.84), channel_id=1, source_target_pairs={{0,3},{1,0},{2,1},{3,2},{4,7},{5,4},{6,5},{7,6},{8,11},{9,8},{10,9... | collective-permute-start | bytes 393224 | tf_op jit(solution)/shard_map/ppermute | solution.py:22
  134.3 7.8 %collective-permute-start.26 = (bf16[128,512]{1,0:T(8,128)(2,1)S(1)}, bf16[128,512]{1,0:T(8,128)(2,1)S(1)}, u32[]{:S(2)}, u32[]{:S(2)}) collective-permute-start(bf16[128,512]{1,0:T(8,128)(2,1)S(1)} %get-tuple-element.79), channel_id=1, source_target_pairs={{0,3},{1,0},{2,1},{3,2},{4,7},{5,4},{6,5},{7,6},{8,11},{9,8},{10,9... | collective-permute-start | bytes 393224 | tf_op jit(solution)/shard_map/ppermute | solution.py:22
  138.6 7.7 %collective-permute-start.25 = (bf16[128,512]{1,0:T(8,128)(2,1)S(1)}, bf16[128,512]{1,0:T(8,128)(2,1)S(1)}, u32[]{:S(2)}, u32[]{:S(2)}) collective-permute-start(bf16[128,512]{1,0:T(8,128)(2,1)S(1)} %add.37), channel_id=1, source_target_pairs={{0,1},{1,2},{2,3},{3,0},{4,5},{5,6},{6,7},{7,4},{8,9},{9,10},{10,1... | collective-permute-start | bytes 393224 | tf_op jit(solution)/shard_map/ppermute | solution.py:22
  138.7 9.4 %collective-permute-start.27 = (bf16[128,512]{1,0:T(8,128)(2,1)S(1)}, bf16[128,512]{1,0:T(8,128)(2,1)S(1)}, u32[]{:S(2)}, u32[]{:S(2)}) collective-permute-start(bf16[128,512]{1,0:T(8,128)(2,1)S(1)} %get-tuple-element.82), channel_id=1, source_target_pairs={{0,1},{1,2},{2,3},{3,0},{4,5},{5,6},{6,7},{7,4},{8,9},{9,10},{10,1... | collective-permute-start | bytes 393224 | tf_op jit(solution)/shard_map/ppermute | solution.py:22
  138.8 9.3 %collective-permute-start.29 = (bf16[128,512]{1,0:T(8,128)(2,1)S(1)}, bf16[128,512]{1,0:T(8,128)(2,1)S(1)}, u32[]{:S(2)}, u32[]{:S(2)}) collective-permute-start(bf16[128,512]{1,0:T(8,128)(2,1)S(1)} %add.42), channel_id=1, source_target_pairs={{0,3},{1,0},{2,1},{3,2},{4,7},{5,4},{6,5},{7,6},{8,11},{9,8},{10,9... | collective-permute-start | bytes 393224 | tf_op jit(solution)/shard_map/ppermute | solution.py:22
  (14 other events, 163.8 us)
